TPU v7x, 32 devices: a whole 2x2x4 slice. The times are simulated.
32 devices in a mesh: gx: 2 (over x), gy: 4 (over z), gz: 4 (over y, core).
Axes of the slice: x: 2, y: 2, z: 4, core: 2. Of those that a mesh axis runs over, the one named last changes fastest.
Arguments:
- checkpoint: float32 [64, 256, 1024], P('gx', 'gy', 'gz'), may hold values from -6 to 6
- diffusivity: float32 [64, 256, 1024], P('gx', 'gy', 'gz'), may hold values from 0.1 to 1
- material_scale: float32 [4], replicated, may hold values from 0.5 to 1
- labels: int32 [64, 256, 1024], P('gx', 'gy', 'gz'), may hold values from 0 to 3
- measured: float32 [64, 256, 1024], P('gx', 'gy', 'gz'), may hold values from -6 to 6
- observed: int32 [64, 256, 1024], P('gx', 'gy', 'gz'), may hold values 0 or 1
- adjoint_in: float32 [64, 256, 1024], P('gx', 'gy', 'gz'), may hold values from -4 to 4
Outputs:
- gradient: float32 [64, 256, 1024], P('gx', 'gy', 'gz')
- adjoint_start: float32 [64, 256, 1024], P('gx', 'gy', 'gz')
All inputs are finite; a program needn't handle non-finite values. No bound on the sum of `observed` on one device may be relied on, other than what follows from the above.
Results may differ from a plain program's by a relative error of at most 0.00002.
Values sent between devices are 32-bit elements; how exact they have to be, the bound alone decides.
No kernel may reach another device: no remote copies, remote signals or barrier semaphores. Data moves between devices by JAX's collectives and lax.ppermute only.
A program may use at most 192 MiB of HBM per device.

v0:
```python
import functools

import jax
import jax.numpy as jnp
from jax import lax
from jax.experimental import pallas as pl
from jax.experimental.pallas import tpu as pltpu
from jax.sharding import PartitionSpec as P

ITERS = 4
MATERIALS = 4
HALO = ITERS
HALF_RATE = 0.5 * 0.15
ROWS = 80
OWN = 8
GROUPS = 4
BLOCK = 128 // GROUPS
F32 = jnp.float32

in_vmem = pl.BlockSpec(memory_space=pltpu.VMEM)
in_smem = pl.BlockSpec(memory_space=pltpu.SMEM)


def params():
    return pltpu.CompilerParams(vmem_limit_bytes=12 << 20)


def vm(*shape):
    return pltpu.VMEM(shape, F32)


def lanes():
    return lax.broadcasted_iota(jnp.int32, (8, 128), 1)


def sublanes():
    return lax.broadcasted_iota(jnp.int32, (8, 128), 0)


def each(fn, *lists):
    return [fn(*items) for items in zip(*lists)]


def add(a, b):
    return each(lambda x, y: x + y, a, b)


def sub(a, b):
    return each(lambda x, y: x - y, a, b)


def mul(a, b):
    return each(lambda x, y: x * y, a, b)


def load(ref, x, row, tiles):
    return [ref[x * tiles + t, pl.ds(row, 8), :] for t in range(tiles)]


def store(ref, x, row, values):
    for t, value in enumerate(values):
        ref[x * len(values) + t, pl.ds(row, 8), :] = value


def ahead(values):
    rolled = [pltpu.roll(v, 127, axis=1) for v in values]
    count = len(values)
    if count == 1:
        return rolled
    last = lanes() == 127
    return [jnp.where(last, rolled[(t + 1) % count], rolled[t]) for t in range(count)]


def behind(values):
    rolled = [pltpu.roll(v, 1, axis=1) for v in values]
    count = len(values)
    if count == 1:
        return rolled
    first = lanes() == 0
    return [jnp.where(first, rolled[(t - 1) % count], rolled[t]) for t in range(count)]


class Plan:
    def __init__(self, mesh, shape):
        self.sizes = {axis: mesh.shape[axis] for axis in ("gx", "gy", "gz")}
        self.nx = shape[0] // self.sizes["gx"]
        self.ny = shape[1] // self.sizes["gy"]
        self.nz = shape[2] // self.sizes["gz"]
        self.tiles = self.nz // 128
        self.two_sided = self.sizes["gx"] > 2
        self.deep = self.nx + HALO * (2 if self.two_sided else 1)
        self.planes = self.deep + 2
        self.per_group = self.deep // GROUPS
        self.edge_planes = self.per_group + 2
        self.row_tiles = [OWN - HALO + 8 * t for t in range((self.ny + 2 * HALO) // 8)]
        self.own_tiles = [OWN + 8 * t for t in range(self.ny // 8)]
        self.unroll = 4 if self.two_sided else 3
        self.edge_vregs = self.per_group * len(self.row_tiles)
        self.face_vregs = -(-self.edge_vregs // 4)

    def index(self, axis):
        return lax.axis_index(axis)

    def even(self, axis):
        return lax.rem(lax.axis_index(axis), 2) == 0

    def first(self, axis):
        return lax.axis_index(axis) == 0

    def last(self, axis):
        return lax.axis_index(axis) == self.sizes[axis] - 1

    def own_plane(self):
        if self.two_sided:
            return jnp.int32(1 + HALO)
        return jnp.where(self.even("gx"), 1, 1 + HALO)

    def span(self, step):
        unroll = self.unroll
        if step == ITERS - 1 and self.two_sided:
            return self.own_plane(), self.nx
        if self.two_sided:
            return 1, self.deep
        need = self.nx + HALO - 1 - step
        count = -(-need // unroll) * unroll
        return jnp.where(self.even("gx"), 1, 1 + self.deep - count), count

    def row_keep(self, row):
        if row < OWN:
            return (sublanes() >= OWN - row) | jnp.logical_not(self.first("gy"))
        if row + 8 > OWN + self.ny:
            return (sublanes() < OWN + self.ny - row) | jnp.logical_not(self.last("gy"))
        return None

    def edge_keep(self):
        pos = lanes() % BLOCK
        low = (pos >= 16) & (pos < 20) & self.first("gz")
        high = (pos >= 12) & (pos < 16) & self.last("gz")
        return jnp.logical_not(low | high)


def pairs(count, second):
    if not second:
        return [(i, i ^ 1) for i in range(count)]
    inner = [(i, i + 1) for i in range(1, count - 1, 2)]
    return inner + [(b, a) for a, b in inner]


def swap(plan, axis, first, second, wrap):
    count = plan.sizes[axis]
    got = lax.ppermute(first, axis, pairs(count, False))
    if count == 2:
        return got, got
    ends = [(0, count - 1), (count - 1, 0)] if wrap else [(0, 0), (count - 1, count - 1)]
    return got, lax.ppermute(second, axis, pairs(count, True) + ends)


def send_faces(plan, fields, px, px2, pya, pyb):
    nt = plan.tiles
    own = plan.own_plane()
    even_x, even_y = plan.even("gx"), plan.even("gy")
    wide = HALO * nt
    rows = pl.ds(OWN, plan.ny)
    low, high = own * nt, (own + plan.nx - HALO) * nt
    for f, field in enumerate(fields):
        at = jnp.where(even_x, high, low)
        for j in range(wide):
            px[f * wide + j] = field[at + j, rows, :]
        if plan.two_sided:
            at = jnp.where(even_x, low, high)
            for j in range(wide):
                px2[f * wide + j] = field[at + j, rows, :]
    top = OWN + plan.ny - HALO

    def body(x, _):
        for f, field in enumerate(fields):
            for t in range(nt):
                a = field[(own + x) * nt + t, pl.ds(OWN, HALO), :]
                b = field[(own + x) * nt + t, pl.ds(top, HALO), :]
                if len(fields) == 2:
                    to = (x * nt + t, pl.ds(HALO * f, HALO))
                else:
                    to = (x * (nt // 2) + t // 2, pl.ds(HALO * (t % 2), HALO))
                pya[to[0], to[1], :] = jnp.where(even_y, b, a)
                pyb[to[0], to[1], :] = jnp.where(even_y, a, b)
        return 0

    lax.fori_loop(0, plan.nx, body, 0, unroll=4)


def corner_kernel(plan, per, ya, yb, out, out2):
    even = plan.even("gx")
    low, high = 0, (plan.nx - HALO) * per
    width = HALO * per
    at = jnp.where(even, high, low)
    for n, ref in enumerate((ya, yb)):
        out[n * width : (n + 1) * width] = ref[pl.ds(at, width)]
    if plan.two_sided:
        at = jnp.where(even, low, high)
        for n, ref in enumerate((ya, yb)):
            out2[n * width : (n + 1) * width] = ref[pl.ds(at, width)]


def place_halos(plan, fields, xa, xb, ya, yb, ca, cb):
    nt = plan.tiles
    own = plan.own_plane()
    wide = HALO * nt
    even_x, even_y = plan.even("gx"), plan.even("gy")
    two = len(fields) == 2
    per = nt if two else nt // 2
    below, above = own - HALO, own + plan.nx
    rows = pl.ds(OWN, plan.ny)

    def put_rows(plane, source_a, source_b, at, blank):
        for f, field in enumerate(fields):
            for t in range(nt):
                if two:
                    a = source_a[at + t, pl.ds(HALO * f, HALO), :]
                    b = source_b[at + t, pl.ds(HALO * f, HALO), :]
                else:
                    a = source_a[at + t // 2, pl.ds(HALO * (t % 2), HALO), :]
                    b = source_b[at + t // 2, pl.ds(HALO * (t % 2), HALO), :]
                low = jnp.where(even_y, b, a)
                high = jnp.where(even_y, a, b)
                low = jnp.where(plan.first("gy") | blank, 0.0, low)
                high = jnp.where(plan.last("gy") | blank, 0.0, high)
                field[plane * nt + t, pl.ds(OWN - HALO, HALO), :] = low
                field[plane * nt + t, pl.ds(OWN + plan.ny, HALO), :] = high

    def body(x, _):
        put_rows(own + x, ya, yb, x * per, False)
        return 0

    lax.fori_loop(0, plan.nx, body, 0, unroll=4)

    sides = [(xa, ca, jnp.where(even_x, above, below), False)]
    if plan.two_sided:
        sides[0] = (xa, ca, jnp.where(even_x, above, below), False)
        ends = (even_x & plan.first("gx")) | (jnp.logical_not(even_x) & plan.last("gx"))
        sides.append((xb, cb, jnp.where(even_x, below, above), ends))
    for x_ref, c_ref, plane, blank in sides:
        for f, field in enumerate(fields):
            for j in range(wide):
                value = x_ref[f * wide + j]
                if blank is not False:
                    value = jnp.where(blank, 0.0, value)
                field[plane * nt + j, rows, :] = value
        half = HALO * per
        for j in range(HALO):
            put_rows(plane + j, c_ref.at[pl.ds(0, half)], c_ref.at[pl.ds(half, half)], j * per, blank)
    zero = jnp.zeros((ROWS, 128), F32)
    for field in fields:
        for t in range(nt):
            field[t] = zero
            field[(plan.planes - 1) * nt + t] = zero


def pack_edges(plan, field, edge, row_tiles):
    nt = plan.tiles
    masks = [lanes() >= 16 * j for j in range(2 * GROUPS)]

    def body(i, _):
        for row in row_tiles:
            value = None
            for g in range(GROUPS):
                plane = (g * plan.per_group + 1 + i) * nt
                right = pltpu.roll(field[plane + nt - 1, pl.ds(row, 8), :], (BLOCK * g + 12) % 128, axis=1)
                left = pltpu.roll(field[plane, pl.ds(row, 8), :], (BLOCK * g + 20) % 128, axis=1)
                value = right if value is None else jnp.where(masks[2 * g], right, value)
                value = jnp.where(masks[2 * g + 1], left, value)
            edge[i + 1, pl.ds(row, 8), :] = value
        return 0

    lax.fori_loop(0, plan.per_group, body, 0)


def edge_places(plan):
    return [(i + 1, row) for i in range(plan.per_group) for row in plan.row_tiles]


def pack_faces(plan, edge, out, base):
    lane = lanes()
    places = edge_places(plan)
    for q in range(plan.face_vregs):
        value = None
        for slot, (i, row) in enumerate(places[4 * q : 4 * q + 4]):
            held = edge[i, pl.ds(row, 8), :]
            low = pltpu.roll(held, (8 * slot - 20) % 128, axis=1)
            high = pltpu.roll(held, (8 * slot - 4) % 128, axis=1)
            both = jnp.where(lane % 8 < 4, low, high)
            value = both if value is None else jnp.where(lane % BLOCK >= 8 * slot, both, value)
        out[base + q] = value


def place_faces(plan, edge, za, zb, base):
    lane = lanes()
    pos = lane % BLOCK
    halo = (pos >= 12) & (pos < 20)
    even = plan.even("gz")
    places = edge_places(plan)
    for q in range(plan.face_vregs):
        a, b = za[base + q], zb[base + q]
        right = jnp.where(plan.last("gz"), 0.0, jnp.where(even, a, b))
        left = jnp.where(plan.first("gz"), 0.0, jnp.where(even, b, a))
        both = jnp.where(lane % 8 < 4, right, left)
        for slot, (i, row) in enumerate(places[4 * q : 4 * q + 4]):
            moved = pltpu.roll(both, (12 - 8 * slot) % 128, axis=1)
            edge[i, pl.ds(row, 8), :] = jnp.where(halo, moved, edge[i, pl.ds(row, 8), :])


def wrap_planes(plan, edge):
    lane = lanes()
    last = plan.per_group
    for row in plan.row_tiles:
        before = pltpu.roll(edge[last, pl.ds(row, 8), :], BLOCK, axis=1)
        after = pltpu.roll(edge[1, pl.ds(row, 8), :], 128 - BLOCK, axis=1)
        edge[0, pl.ds(row, 8), :] = jnp.where(lane < BLOCK, 0.0, before)
        edge[last + 1, pl.ds(row, 8), :] = jnp.where(lane >= 128 - BLOCK, 0.0, after)


def merge_edges(plan, values, edge, plane, row):
    lane = lanes()
    g = (plane - 1) // plan.per_group
    i = plane - g * plan.per_group
    held = edge[i, pl.ds(row, 8), :]
    left = pltpu.roll(held, lax.rem(256 - 20 - BLOCK * g, 128), axis=1)
    right = pltpu.roll(held, lax.rem(256 - 12 - BLOCK * g, 128), axis=1)
    values = list(values)
    values[0] = jnp.where(lane < 4, left, values[0])
    values[-1] = jnp.where(lane >= 124, right, values[-1])
    return values


def face_coefficients(plan, k, cx, cy, cz, czm, planes, tiles):
    def body(x, _):
        for row in plan.row_tiles:
            here = load(k, x, row, tiles)
            store(cx, x, row, add(here, load(k, x + 1, row, tiles)))
            store(cy, x, row, add(here, load(k, x, row + 1, tiles)))
            store(cz, x, row, add(here, ahead(here)))
            store(czm, x, row, add(here, behind(here)))
        return 0

    lax.fori_loop(0, planes - 1, body, 0, unroll=2)


def step_forward(plan, v, w, c, start, count, unroll, row_tiles, tiles, keep, plane_keep):
    cx, cy, cz, czm = c

    def body(i, _):
        first = start + i * unroll
        for row in row_tiles:
            here = load(v, first, row, tiles)
            flow = mul(load(cx, first - 1, row, tiles), sub(here, load(v, first - 1, row, tiles)))
            for k in range(unroll):
                x = first + k
                after = load(v, x + 1, row, tiles)
                out = mul(load(cx, x, row, tiles), sub(after, here))
                total = add(here, sub(out, flow))
                flow = out
                up = mul(load(cy, x, row, tiles), sub(load(v, x, row + 1, tiles), here))
                down = mul(load(cy, x, row - 1, tiles), sub(here, load(v, x, row - 1, tiles)))
                total = add(total, sub(up, down))
                right = mul(load(cz, x, row, tiles), sub(ahead(here), here))
                left = mul(load(czm, x, row, tiles), sub(here, behind(here)))
                total = add(total, sub(right, left))
                store(w, x, row, kept(plan, total, row, keep, plane_keep, x))
                here = after
        return 0

    lax.fori_loop(0, count // unroll, body, 0)


def kept(plan, total, row, keep, plane_keep, x):
    mask = plan.row_keep(row)
    if keep is not None:
        mask = keep if mask is None else mask & keep
    if plane_keep is not None:
        inside = plane_keep(x)
        mask = inside if mask is None else mask & inside
    if mask is None:
        return total
    return [jnp.where(mask, value, 0.0) for value in total]


def step_backward(plan, v, w, u, acc, ay, az, c, start, count, unroll, row_tiles, tiles, keep, plane_keep, fresh):
    cx, cy, cz, czm = c

    def body(i, _):
        first = start + i * unroll
        for row in row_tiles:
            here = load(v, first, row, tiles)
            temp = load(u, first, row, tiles)
            diff = sub(here, load(v, first - 1, row, tiles))
            flow = mul(load(cx, first - 1, row, tiles), diff)
            part = mul(diff, sub(temp, load(u, first - 1, row, tiles)))
            for k in range(unroll):
                x = first + k
                after, temp_after = load(v, x + 1, row, tiles), load(u, x + 1, row, tiles)
                diff = sub(after, here)
                out = mul(load(cx, x, row, tiles), diff)
                total = add(here, sub(out, flow))
                flow = out
                term = mul(diff, sub(temp_after, temp))
                both = add(part, term)
                part = term
                store(acc, x, row, both if fresh else add(both, load(acc, x, row, tiles)))
                diff = sub(load(v, x, row + 1, tiles), here)
                up = mul(load(cy, x, row, tiles), diff)
                down = mul(load(cy, x, row - 1, tiles), sub(here, load(v, x, row - 1, tiles)))
                total = add(total, sub(up, down))
                term = mul(diff, sub(load(u, x, row + 1, tiles), temp))
                store(ay, x, row, term if fresh else add(term, load(ay, x, row, tiles)))
                diff = sub(ahead(here), here)
                right = mul(load(cz, x, row, tiles), diff)
                left = mul(load(czm, x, row, tiles), sub(here, behind(here)))
                total = add(total, sub(right, left))
                term = mul(diff, sub(ahead(temp), temp))
                store(az, x, row, term if fresh else add(term, load(az, x, row, tiles)))
                store(w, x, row, kept(plan, total, row, keep, plane_keep, x))
                here, temp = after, temp_after
        return 0

    lax.fori_loop(0, count // unroll, body, 0)


def plane_keeper(plan):
    if not plan.two_sided:
        return None
    low = jnp.where(plan.first("gx"), 1 + HALO, 0)
    high = jnp.where(plan.last("gx"), 1 + HALO + plan.nx, plan.planes)
    return lambda x: (x >= low) & (x < high)


def clear_ends(plan, fields):
    zero = jnp.zeros((ROWS, 128), F32)
    nt = plan.tiles
    for field in fields:
        for t in range(nt):
            field[t] = zero
            field[(plan.planes - 1) * nt + t] = zero


def start_kernel(plan, scale, u0, diffusivity, labels, u, k, px, pya, pyb, *px2):
    nt = plan.tiles
    own = plan.own_plane()
    values = [scale[m] for m in range(MATERIALS)]

    def body(x, _):
        for t in range(nt):
            cols = pl.ds(128 * t, 128)
            u[(own + x) * nt + t, pl.ds(OWN, plan.ny), :] = u0[x, :, cols]
            k[(own + x) * nt + t, pl.ds(OWN, plan.ny), :] = (
                diffusivity[x, :, cols] * factor_of(labels[x, :, cols], values) * HALF_RATE
            )
        return 0

    lax.fori_loop(0, plan.nx, body, 0, unroll=2)
    send_faces(plan, (u, k), px, px2[0] if px2 else None, pya, pyb)


def factor_of(labels, values):
    out = jnp.zeros(labels.shape, F32) + values[0]
    for m in range(1, MATERIALS):
        out = jnp.where(labels == m, values[m], out)
    return out


def ready_kernel(plan, u, k, xa, xb, ya, yb, ca, cb, u_out, k_out, cx, cy, cz, czm, eu, ek, pz):
    del u, k
    place_halos(plan, (u_out, k_out), xa, xb, ya, yb, ca, cb)
    face_coefficients(plan, k_out, cx, cy, cz, czm, plan.planes, plan.tiles)
    pack_edges(plan, u_out, eu, plan.row_tiles)
    pack_edges(plan, k_out, ek, plan.row_tiles)
    pack_faces(plan, eu, pz, 0)
    pack_faces(plan, ek, pz, plan.face_vregs)


def forward_kernel(plan, u0, cx, cy, cz, czm, u1, u2, u3, u4):
    fields = (u0, u1, u2, u3, u4)
    clear_ends(plan, fields[1:ITERS])
    keeper = plane_keeper(plan)
    for n in range(ITERS):
        start, count = plan.span(n)
        tiles = plan.own_tiles if n == ITERS - 1 else plan.row_tiles
        step_forward(plan, fields[n], fields[n + 1], (cx, cy, cz, czm), start, count, plan.unroll, tiles, plan.tiles, None, keeper)


def edge_forward_kernel(plan, eu, ek, za, zb, e0, u1, u2, u3, u4, cx, cy, cz, czm, k):
    e0[...] = eu[...]
    k[...] = ek[...]
    place_faces(plan, e0, za, zb, 0)
    place_faces(plan, k, za, zb, plan.face_vregs)
    wrap_planes(plan, e0)
    wrap_planes(plan, k)
    face_coefficients(plan, k, cx, cy, cz, czm, plan.edge_planes, 1)
    keep = plan.edge_keep()
    keeper = edge_keeper(plan)
    fields = (e0, u1, u2, u3, u4)
    for n in range(ITERS):
        step_forward(plan, fields[n], fields[n + 1], (cx, cy, cz, czm), 1, plan.per_group, edge_unroll(plan), plan.row_tiles, 1, keep, keeper)
        wrap_planes(plan, fields[n + 1])


def edge_unroll(plan):
    return 3 if plan.per_group % 3 == 0 else 2


def edge_keeper(plan):
    group = lanes() // BLOCK
    low = jnp.where(plan.first("gx"), plan.own_plane(), 1)
    high = jnp.where(plan.last("gx"), plan.own_plane() + plan.nx, plan.planes)

    def inside(i):
        plane = group * plan.per_group + i
        return (plane >= low) & (plane < high)

    return inside if plan.two_sided else None


def middle_kernel(plan, u4, e4, measured, observed, adjoint, lam, px, pya, pyb, *px2):
    nt = plan.tiles
    own = plan.own_plane()

    def body(x, _):
        for row in plan.own_tiles:
            temp = merge_edges(plan, load(u4, own + x, row, nt), e4, own + x, row)
            for t in range(nt):
                at = (x, pl.ds(row - OWN, 8), pl.ds(128 * t, 128))
                temp[t] = adjoint[at] + observed[at].astype(F32) * (temp[t] - measured[at])
            store(lam, own + x, row, temp)
        return 0

    lax.fori_loop(0, plan.nx, body, 0, unroll=2)
    send_faces(plan, (lam,), px, px2[0] if px2 else None, pya, pyb)


def turn_kernel(plan, lam, xa, xb, ya, yb, ca, cb, lam_out, edge, pz):
    del lam
    place_halos(plan, (lam_out,), xa, xb, ya, yb, ca, cb)
    pack_edges(plan, lam_out, edge, plan.row_tiles)
    pack_faces(plan, edge, pz, 0)


def backward_kernel(plan, lam, u0, u1, u2, u3, cx, cy, cz, czm, w, other, acc, ay, az):
    fields = (u0, u1, u2, u3)
    clear_ends(plan, (w, other))
    keeper = plane_keeper(plan)
    nt = plan.tiles
    buffers = [lam, other, w, other, w]
    for m in range(ITERS):
        start, count = plan.span(m)
        tiles = plan.own_tiles if m == ITERS - 1 else plan.row_tiles
        n = ITERS - 1 - m
        step_backward(
            plan, buffers[m], buffers[m + 1], fields[n], acc, ay, az, (cx, cy, cz, czm),
            start, count, plan.unroll, tiles, nt, None, keeper, m == 0,
        )
    own = plan.own_plane()

    def body(x, _):
        at, row = own + x, OWN - 8
        v, u = buffers[ITERS - 1], fields[0]
        term = mul(
            sub(load(v, at, row + 1, nt), load(v, at, row, nt)),
            sub(load(u, at, row + 1, nt), load(u, at, row, nt)),
        )
        for t in range(nt):
            ay[at * nt + t, pl.ds(OWN - 1, 1), :] += term[t][7:8]
        return 0

    lax.fori_loop(0, plan.nx, body, 0, unroll=4)


def edge_backward_kernel(plan, lam, za, zb, u0, u1, u2, u3, cx, cy, cz, czm, w, total, e, other, acc, ay, az):
    e[...] = lam[...]
    place_faces(plan, e, za, zb, 0)
    wrap_planes(plan, e)
    keep = plan.edge_keep()
    keeper = edge_keeper(plan)
    fields = (u0, u1, u2, u3)
    buffers = [e, other, w, other, w]
    for m in range(ITERS):
        n = ITERS - 1 - m
        step_backward(
            plan, buffers[m], buffers[m + 1], fields[n], acc, ay, az, (cx, cy, cz, czm),
            1, plan.per_group, edge_unroll(plan), plan.row_tiles, 1, keep, keeper, m == 0,
        )
        if m < ITERS - 1:
            wrap_planes(plan, buffers[m + 1])

    def body(i, _):
        for row in plan.own_tiles:
            z = [az[i + 1, pl.ds(row, 8), :]]
            whole = acc[i + 1, pl.ds(row, 8), :] + ay[i + 1, pl.ds(row, 8), :] + ay[i + 1, pl.ds(row - 1, 8), :]
            total[i + 1, pl.ds(row, 8), :] = whole + z[0] + behind(z)[0]
        return 0

    lax.fori_loop(0, plan.per_group, body, 0)


def finish_kernel(plan, scale, labels, lam, acc, ay, az, e_lam, e_total, gradient, adjoint):
    nt = plan.tiles
    own = plan.own_plane()
    values = [scale[m] for m in range(MATERIALS)]

    def body(x, _):
        p = own + x
        for row in plan.own_tiles:
            z = load(az, p, row, nt)
            total = add(load(acc, p, row, nt), add(load(ay, p, row, nt), load(ay, p, row - 1, nt)))
            total = add(total, add(z, behind(z)))
            total = merge_edges(plan, total, e_total, p, row)
            end = merge_edges(plan, load(lam, p, row, nt), e_lam, p, row)
            for t in range(nt):
                at = (x, pl.ds(row - OWN, 8), pl.ds(128 * t, 128))
                gradient[at] = total[t] * (-HALF_RATE) * factor_of(labels[at], values)
                adjoint[at] = end[t]
        return 0

    lax.fori_loop(0, plan.nx, body, 0, unroll=2)


def call(kernel, plan, outs, args, alias=None, scratch=(), smem=0, flops=0):
    specs = [in_smem] * smem + [in_vmem] * (len(args) - smem)
    cost = pl.CostEstimate(flops=flops, bytes_accessed=flops, transcendentals=0) if flops else None
    return pl.pallas_call(
        functools.partial(kernel, plan),
        out_shape=tuple(outs),
        in_specs=specs,
        out_specs=(in_vmem,) * len(outs),
        input_output_aliases=alias or {},
        scratch_shapes=list(scratch),
        cost_estimate=cost,
        compiler_params=params(),
        name=kernel.__name__,
    )(*args)


def shards(plan, checkpoint, diffusivity, material_scale, labels, measured, observed, adjoint_in):
    nt = plan.tiles
    work = vm(plan.planes * nt, ROWS, 128)
    edge = vm(plan.edge_planes, ROWS, 128)
    wide = HALO * nt

    def faces(count):
        x = vm(count * wide, plan.ny, 128)
        y = vm(plan.nx * nt * count // 2, 2 * HALO, 128)
        return (x, y, y) + ((x,) if plan.two_sided else ())

    def exchange(count, sent):
        px, pya, pyb = sent[:3]
        px2 = sent[3] if plan.two_sided else None
        xa, xb = swap(plan, "gx", px, px2, False)
        ya, yb = swap(plan, "gy", pya, pyb, False)
        per = nt * count // 2
        corner = vm(2 * HALO * per, 2 * HALO, 128)
        body = functools.partial(corner_kernel, plan, per)
        if plan.two_sided:
            shapes, fn = (corner, corner), body
        else:
            shapes, fn = (corner,), lambda ya, yb, out: body(ya, yb, out, None)
        corners = pl.pallas_call(
            fn, out_shape=shapes, in_specs=[in_vmem] * 2, out_specs=(in_vmem,) * len(shapes),
            compiler_params=params(), name="corner_kernel",
        )(ya, yb)
        ca, cb = swap(plan, "gx", corners[0], corners[-1], False)
        return xa, xb, ya, yb, ca, cb

    u, k, *sent = call(start_kernel, plan, (work, work) + faces(2), (material_scale, checkpoint, diffusivity, labels), smem=1)
    got = exchange(2, sent)
    u, k, cx, cy, cz, czm, eu, ek, pz = call(
        ready_kernel, plan, (work, work, work, work, work, work, edge, edge, vm(2 * plan.face_vregs, 8, 128)),
        (u, k) + got, alias={0: 0, 1: 1},
    )
    c = (cx, cy, cz, czm)
    za, zb = swap(plan, "gz", pz, pz, True)
    u1, u2, u3, u4 = call(forward_kernel, plan, (work,) * 4, (u,) + c, flops=1 << 24)
    e0, e1, e2, e3, e4, ex, ey, ez, ezm = call(edge_forward_kernel, plan, (edge,) * 9, (eu, ek, za, zb), scratch=(edge,))
    lam, *sent = call(middle_kernel, plan, (work,) + faces(1), (u4, e4, measured, observed, adjoint_in))
    got = exchange(1, sent)
    lam, e_lam, pz = call(turn_kernel, plan, (work, edge, vm(plan.face_vregs, 8, 128)), (lam,) + got, alias={0: 0})
    za, zb = swap(plan, "gz", pz, pz, True)
    start, _, acc, ay, az = call(backward_kernel, plan, (work,) * 5, (lam, u, u1, u2, u3) + c, flops=1 << 25)
    e_start, e_total = call(
        edge_backward_kernel, plan, (edge,) * 2, (e_lam, za, zb, e0, e1, e2, e3, ex, ey, ez, ezm), scratch=(edge,) * 5
    )
    block = jax.ShapeDtypeStruct((plan.nx, plan.ny, plan.nz), F32)
    return call(finish_kernel, plan, (block, block), (material_scale, labels, start, acc, ay, az, e_start, e_total), smem=1)


def solution(mesh):
    spec = P("gx", "gy", "gz")

    def run(*args):
        plan = Plan(mesh, args[0].shape)
        return jax.shard_map(
            functools.partial(shards, plan),
            mesh=mesh,
            in_specs=(spec, spec, P(), spec, spec, spec, spec),
            out_specs=(spec, spec),
            check_vma=False,
        )(*args)

    return run
```

profile of v0, /device:TPU:9, one launch (start us, length us, event | category | flops | bytes accessed | tf_op | source)
XLA Modules:
  0.0 89.2 jit_solution(7278494071065247851)
XLA Ops:
  0.6 0.0 copy-start.6
  0.6 1.6 %copy-done.6 = s32[32,64,256]{2,1,0:T(8,128)S(1)} copy-done((s32[32,64,256]{2,1,0:T(8,128)S(1)}, s32[32,64,256]{2,1,0:T(8,128)}, u32[]{:S(2)}) %copy-start.6) | copy-done | bytes 2097176
  2.2 0.0 copy-start.8
  2.2 1.6 %copy-done.8 = f32[32,64,256]{2,1,0:T(8,128)S(1)} copy-done((f32[32,64,256]{2,1,0:T(8,128)S(1)}, f32[32,64,256]{2,1,0:T(8,128)}, u32[]{:S(2)}) %copy-start.8) | copy-done | bytes 2097176
  3.8 0.0 copy-start.9
  3.8 1.6 %copy-done.9 = f32[32,64,256]{2,1,0:T(8,128)S(1)} copy-done((f32[32,64,256]{2,1,0:T(8,128)S(1)}, f32[32,64,256]{2,1,0:T(8,128)}, u32[]{:S(2)}) %copy-start.9) | copy-done | bytes 2097176
  5.4 0.0 copy-start.13
  5.4 0.7 copy-done.13
  6.1 1.4 %start_kernel.1 = (f32[76,80,128]{2,1,0:T(8,128)S(1)}, f32[76,80,128]{2,1,0:T(8,128)S(1)}, f32[16,64,128]{2,1,0:T(8,128)S(1)}, f32[64,8,128]{2,1,0:T(8,128)S(1)}, f32[64,8,128]{2,1,0:T(8,128)S(1)}) custom-call(f32[4]{0:T(128)S(1)} %copy-done.13, f32[32,64,256]{2,1,0:T(8,128)S(1)} %copy-done.8, f32[32,64,256]{2,1,0:T(8,128)S(1)} %copy-done.9, ...), custom_call_target="tpu_custom_call" | custom-call | tf_op jit(solution)/shard_map/start_kernel/pallas_call | solution.py:627
  7.5 1.3 %collective-permute-start = (f32[16,64,128]{2,1,0:T(8,128)S(1)}, f32[16,64,128]{2,1,0:T(8,128)S(1)}, u32[]{:S(2)}, u32[]{:S(2)}) collective-permute-start(f32[16,64,128]{2,1,0:T(8,128)S(1)} %get-tuple-element.43), channel_id=1, source_target_pairs={{0,16},{16,0},{1,17},{17,1},{2,18},{18,2},{3,19},{19,3},{4,20},{20... | collective-permute-start | bytes 1572872 | tf_op jit(solution)/shard_map/ppermute | solution.py:151
  8.7 0.2 collective-permute-start.1
  8.9 4.3 %collective-permute-start.2 = (f32[64,8,128]{2,1,0:T(8,128)S(1)}, f32[64,8,128]{2,1,0:T(8,128)S(1)}, u32[]{:S(2)}, u32[]{:S(2)}) collective-permute-start(f32[64,8,128]{2,1,0:T(8,128)S(1)} %get-tuple-element.45), channel_id=1, source_target_pairs={{4,8},{8,4},{0,0},{12,12},{5,9},{9,5},{1,1},{13,13},{6,10},{10,6},... | collective-permute-start | bytes 786440 | tf_op jit(solution)/shard_map/ppermute | solution.py:155
  13.2 2.4 %collective-permute-done.1.ya = f32[64,8,128]{2,1,0:T(8,128)S(1)} collective-permute-done((f32[64,8,128]{2,1,0:T(8,128)S(1)}, f32[64,8,128]{2,1,0:T(8,128)S(1)}, u32[]{:S(2)}, u32[]{:S(2)}) %collective-permute-start.1) | collective-permute-done | bytes 262176 | tf_op jit(solution)/shard_map/ppermute | solution.py:151
  15.6 3.0 %collective-permute-done.2.yb = f32[64,8,128]{2,1,0:T(8,128)S(1)} collective-permute-done((f32[64,8,128]{2,1,0:T(8,128)S(1)}, f32[64,8,128]{2,1,0:T(8,128)S(1)}, u32[]{:S(2)}, u32[]{:S(2)}) %collective-permute-start.2) | collective-permute-done | bytes 262176 | tf_op jit(solution)/shard_map/ppermute | solution.py:155
  18.6 0.3 collective-permute-start.3
  18.9 3.0 %collective-permute-done.3.ca.cb = f32[16,8,128]{2,1,0:T(8,128)S(1)} collective-permute-done((f32[16,8,128]{2,1,0:T(8,128)S(1)}, f32[16,8,128]{2,1,0:T(8,128)S(1)}, u32[]{:S(2)}, u32[]{:S(2)}) %collective-permute-start.3) | collective-permute-done | bytes 65568 | tf_op jit(solution)/shard_map/ppermute | solution.py:151
  21.9 0.0 collective-permute-done.xa.xb
  21.9 5.9 %ready_kernel.1 = (f32[76,80,128]{2,1,0:T(8,128)S(1)}, f32[76,80,128]{2,1,0:T(8,128)S(1)}, f32[76,80,128]{2,1,0:T(8,128)S(1)}, f32[76,80,128]{2,1,0:T(8,128)S(1)...) custom-call(f32[76,80,128]{2,1,0:T(8,128)S(1)} %get-tuple-element.41, ...), custom_call_target="tpu_custom_call", output_to_operand_aliasing={{0}: (0, {}), {1}: (1, {})} | custom-call | tf_op jit(solution)/shard_map/ready_kernel/pallas_call | solution.py:627
  27.8 0.0 copy-start
  27.8 0.0 copy-start.2
  27.8 0.0 copy-start.4
  27.9 2.9 %collective-permute-start.4 = (f32[42,8,128]{2,1,0:T(8,128)S(1)}, f32[42,8,128]{2,1,0:T(8,128)S(1)}, u32[]{:S(2)}, u32[]{:S(2)}) collective-permute-start(f32[42,8,128]{2,1,0:T(8,128)S(1)} %get-tuple-element.54), channel_id=1, source_target_pairs={{0,1},{1,0},{2,3},{3,2},{4,5},{5,4},{6,7},{7,6},{8,9},{9,8},{10,11... | collective-permute-start | bytes 516104 | tf_op jit(solution)/shard_map/ppermute | solution.py:151
  30.8 1.2 %collective-permute-start.5 = (f32[42,8,128]{2,1,0:T(8,128)S(1)}, f32[42,8,128]{2,1,0:T(8,128)S(1)}, u32[]{:S(2)}, u32[]{:S(2)}) collective-permute-start(f32[42,8,128]{2,1,0:T(8,128)S(1)} %get-tuple-element.54), channel_id=1, source_target_pairs={{1,2},{2,1},{0,3},{3,0},{5,6},{6,5},{4,7},{7,4},{9,10},{10,9},{8,1... | collective-permute-start | bytes 516104 | tf_op jit(solution)/shard_map/ppermute | solution.py:155
  32.0 0.0 copy-start.10
  32.0 0.0 copy-start.11
  32.0 0.0 copy-start.12
  32.0 10.1 %forward_kernel.1 = (f32[76,80,128]{2,1,0:T(8,128)S(1)}, f32[76,80,128]{2,1,0:T(8,128)S(1)}, f32[76,80,128]{2,1,0:T(8,128)S(1)}, f32[76,80,128]{2,1,0:T(8,128)S(1)}) custom-call(f32[76,80,128]{2,1,0:T(8,128)S(1)} %get-tuple-element.46.u0, f32[76,80,128]{2,1,0:T(8,128)S(1)} %get-tuple-element.47.cx, f32[76,80,128]{2,1,0:T(8,128)S(1)} %get-tuple-element.48.cy, ...), custom_call_target="tpu_custom_call" | custom-call | flops 16777216 | bytes 16777216 | tf_op jit(solution)/shard_map/forward_kernel/pallas_call | solution.py:627
  42.1 0.0 copy-done
  42.1 0.0 copy-done.2
  42.1 0.0 copy-done.4
  42.1 0.0 collective-permute-done.4.za
  42.1 0.0 collective-permute-done.5.zb
  42.1 2.9 %edge_forward_kernel.1 = (f32[11,80,128]{2,1,0:T(8,128)S(1)}, f32[11,80,128]{2,1,0:T(8,128)S(1)}, f32[11,80,128]{2,1,0:T(8,128)S(1)}, f32[11,80,128]{2,1,0:T(8,1...) custom-call(f32[11,80,128]{2,1,0:T(8,128)S(1)} %get-tuple-element.52, ...), custom_call_target="tpu_custom_call" | custom-call | tf_op jit(solution)/shard_map/edge_forward_kernel/pallas_call | solution.py:627
  45.0 0.0 copy-done.10
  45.1 0.0 copy-done.11
  45.1 0.0 copy-done.12
  45.1 0.0 copy-start.5
  45.1 1.9 %middle_kernel.1 = (f32[76,80,128]{2,1,0:T(8,128)S(1)}, f32[8,64,128]{2,1,0:T(8,128)S(1)}, f32[32,8,128]{2,1,0:T(8,128)S(1)}, f32[32,8,128]{2,1,0:T(8,128)S(1)}) custom-call(f32[76,80,128]{2,1,0:T(8,128)S(1)} %get-tuple-element.51.u4, f32[11,80,128]{2,1,0:T(8,128)S(1)} %get-tuple-element.55.e4, f32[32,64,256]{2,1,0:T(8,128)S(1)} %copy-done.10, ...), custom_call_target="tpu_custom_call" | custom-call | tf_op jit(solution)/shard_map/middle_kernel/pallas_call | solution.py:627
  47.0 0.0 copy-start.1
  47.0 0.3 collective-permute-start.6
  47.4 0.0 collective-permute-start.7
  47.4 4.0 %collective-permute-start.8 = (f32[32,8,128]{2,1,0:T(8,128)S(1)}, f32[32,8,128]{2,1,0:T(8,128)S(1)}, u32[]{:S(2)}, u32[]{:S(2)}) collective-permute-start(f32[32,8,128]{2,1,0:T(8,128)S(1)} %get-tuple-element.59), channel_id=1, source_target_pairs={{4,8},{8,4},{0,0},{12,12},{5,9},{9,5},{1,1},{13,13},{6,10},{10,6},... | collective-permute-start | bytes 393224 | tf_op jit(solution)/shard_map/ppermute | solution.py:155
  51.3 0.3 collective-permute-done.7.ya
  51.7 2.5 %collective-permute-done.8.yb = f32[32,8,128]{2,1,0:T(8,128)S(1)} collective-permute-done((f32[32,8,128]{2,1,0:T(8,128)S(1)}, f32[32,8,128]{2,1,0:T(8,128)S(1)}, u32[]{:S(2)}, u32[]{:S(2)}) %collective-permute-start.8) | collective-permute-done | bytes 131104 | tf_op jit(solution)/shard_map/ppermute | solution.py:155
  54.2 0.6 collective-permute-start.9
  54.8 2.2 %collective-permute-done.9.ca.cb = f32[8,8,128]{2,1,0:T(8,128)S(1)} collective-permute-done((f32[8,8,128]{2,1,0:T(8,128)S(1)}, f32[8,8,128]{2,1,0:T(8,128)S(1)}, u32[]{:S(2)}, u32[]{:S(2)}) %collective-permute-start.9) | collective-permute-done | bytes 32800 | tf_op jit(solution)/shard_map/ppermute | solution.py:151
  56.9 0.0 collective-permute-done.6.xa.xb
  56.9 1.7 %turn_kernel.1 = (f32[76,80,128]{2,1,0:T(8,128)S(1)}, f32[11,80,128]{2,1,0:T(8,128)S(1)}, f32[21,8,128]{2,1,0:T(8,128)S(1)}) custom-call(f32[76,80,128]{2,1,0:T(8,128)S(1)} %get-tuple-element.56.lam, f32[8,64,128]{2,1,0:T(8,128)S(1)} %collective-permute-done.6.xa.xb, ...), custom_call_target="tpu_custom_call", output_to_operand_aliasing={{0}: (0, {})} | custom-call | tf_op jit(solution)/shard_map/turn_kernel/pallas_call | solution.py:627
  58.6 2.8 %collective-permute-start.10 = (f32[21,8,128]{2,1,0:T(8,128)S(1)}, f32[21,8,128]{2,1,0:T(8,128)S(1)}, u32[]{:S(2)}, u32[]{:S(2)}) collective-permute-start(f32[21,8,128]{2,1,0:T(8,128)S(1)} %get-tuple-element.69), channel_id=1, source_target_pairs={{0,1},{1,0},{2,3},{3,2},{4,5},{5,4},{6,7},{7,6},{8,9},{9,8},{10,11... | collective-permute-start | bytes 258056 | tf_op jit(solution)/shard_map/ppermute | solution.py:151
  61.4 0.2 collective-permute-start.11
  61.6 0.0 copy-done.5
  61.6 0.0 copy-done.1
  61.6 0.0 copy-start.3
  61.6 1.9 %copy-done.3 = f32[76,80,128]{2,1,0:T(8,128)S(1)} copy-done((f32[76,80,128]{2,1,0:T(8,128)S(1)}, f32[76,80,128]{2,1,0:T(8,128)}, u32[]{:S(2)}) %copy-start.3) | copy-done | bytes 3112984
  63.5 16.7 %backward_kernel.1 = (f32[76,80,128]{2,1,0:T(8,128)S(1)}, f32[76,80,128]{2,1,0:T(8,128)}, f32[76,80,128]{2,1,0:T(8,128)S(1)}, f32[76,80,128]{2,1,0:T(8,128)S(1)}, f32[76,80,128]{2,1,0:T(8,128)S(1)}) custom-call(f32[76,80,128]{2,1,0:T(8,128)S(1)} %get-tuple-element.60.lam, f32[76,80,128]{2,1,0:T(8,128)S(1)} %get-tuple-element.46.u0, ...), custom_call_target="tpu_custom_call" | custom-call | flops 33554432 | bytes 33554432 | tf_op jit(solution)/shard_map/backward_kernel/pallas_call | solution.py:627
  80.2 0.0 copy-start.7
  80.2 0.0 copy-start.14
  80.2 0.0 collective-permute-done.10.za
  80.2 0.0 collective-permute-done.11.zb
  80.2 3.5 %edge_backward_kernel.1 = (f32[11,80,128]{2,1,0:T(8,128)S(1)}, f32[11,80,128]{2,1,0:T(8,128)S(1)}) custom-call(f32[11,80,128]{2,1,0:T(8,128)S(1)} %get-tuple-element.68.lam, f32[21,8,128]{2,1,0:T(8,128)S(1)} %collective-permute-done.10.za, f32[21,8,128]{2,1,0:T(8,128)S(1)} %collective-permute-done.11.zb, f32[11,80,128]{2,1,0:T(8,128)S(1)} %get-tuple-element.70.u0, ...), custom_call_target="tpu_custom_call" | custom-call | tf_op jit(solution)/shard_map/edge_backward_kernel/pallas_call | solution.py:627
  83.7 0.0 copy-done.7
  83.7 0.0 copy-done.14
  83.7 5.5 %finish_kernel.1 = (f32[32,64,256]{2,1,0:T(8,128)}, f32[32,64,256]{2,1,0:T(8,128)}) custom-call(f32[4]{0:T(128)S(1)} %copy-done.14, s32[32,64,256]{2,1,0:T(8,128)S(1)} %copy-done.7, f32[76,80,128]{2,1,0:T(8,128)S(1)} %get-tuple-element.64.lam, f32[76,80,128]{2,1,0:T(8,128)S(1)} %get-tuple-element.65.acc, f32[76,80,128]{2,1,0:T(8,128)S(1)} %get-tuple-element.66.ay, ...), custom_call_target="tpu_custom_call" | custom-call | tf_op jit(solution)/shard_map/finish_kernel/pallas_call | solution.py:627
  (2 shorter events, 0.0 us)
Async XLA Ops:
  0.6 1.6 %copy-start.6 = (s32[32,64,256]{2,1,0:T(8,128)S(1)}, s32[32,64,256]{2,1,0:T(8,128)}, u32[]{:S(2)}) copy-start(s32[32,64,256]{2,1,0:T(8,128)} %labels.3) | copy-start | bytes 6291460
  2.2 1.6 %copy-start.8 = (f32[32,64,256]{2,1,0:T(8,128)S(1)}, f32[32,64,256]{2,1,0:T(8,128)}, u32[]{:S(2)}) copy-start(f32[32,64,256]{2,1,0:T(8,128)} %u0.1) | copy-start | bytes 6291460
  3.8 1.6 %copy-start.9 = (f32[32,64,256]{2,1,0:T(8,128)S(1)}, f32[32,64,256]{2,1,0:T(8,128)}, u32[]{:S(2)}) copy-start(f32[32,64,256]{2,1,0:T(8,128)} %diffusivity.1) | copy-start | bytes 6291460
  5.4 0.7 copy-start.13
  7.5 14.4 %collective-permute-start = (f32[16,64,128]{2,1,0:T(8,128)S(1)}, f32[16,64,128]{2,1,0:T(8,128)S(1)}, u32[]{:S(2)}, u32[]{:S(2)}) collective-permute-start(f32[16,64,128]{2,1,0:T(8,128)S(1)} %get-tuple-element.43), channel_id=1, source_target_pairs={{0,16},{16,0},{1,17},{17,1},{2,18},{18,2},{3,19},{19,3},{4,20},{20... | collective-permute-start | bytes 1572872 | tf_op jit(solution)/shard_map/ppermute | solution.py:151
  8.7 6.9 %collective-permute-start.1 = (f32[64,8,128]{2,1,0:T(8,128)S(1)}, f32[64,8,128]{2,1,0:T(8,128)S(1)}, u32[]{:S(2)}, u32[]{:S(2)}) collective-permute-start(f32[64,8,128]{2,1,0:T(8,128)S(1)} %get-tuple-element.44), channel_id=1, source_target_pairs={{0,4},{4,0},{8,12},{12,8},{1,5},{5,1},{9,13},{13,9},{2,6},{6,2},{1... | collective-permute-start | bytes 786440 | tf_op jit(solution)/shard_map/ppermute | solution.py:151
  8.9 9.7 %collective-permute-start.2 = (f32[64,8,128]{2,1,0:T(8,128)S(1)}, f32[64,8,128]{2,1,0:T(8,128)S(1)}, u32[]{:S(2)}, u32[]{:S(2)}) collective-permute-start(f32[64,8,128]{2,1,0:T(8,128)S(1)} %get-tuple-element.45), channel_id=1, source_target_pairs={{4,8},{8,4},{0,0},{12,12},{5,9},{9,5},{1,1},{13,13},{6,10},{10,6},... | collective-permute-start | bytes 786440 | tf_op jit(solution)/shard_map/ppermute | solution.py:155
  18.6 3.3 %collective-permute-start.3 = (f32[16,8,128]{2,1,0:T(8,128)S(1)}, f32[16,8,128]{2,1,0:T(8,128)S(1)}, u32[]{:S(2)}, u32[]{:S(2)}) collective-permute-start(f32[16,8,128]{2,1,0:T(8,128)S(1)} %corner_kernel.2), channel_id=1, source_target_pairs={{0,16},{16,0},{1,17},{17,1},{2,18},{18,2},{3,19},{19,3},{4,20},{20... | collective-permute-start | bytes 196616 | tf_op jit(solution)/shard_map/ppermute | solution.py:151
  27.8 14.2 %copy-start = (f32[76,80,128]{2,1,0:T(8,128)}, f32[76,80,128]{2,1,0:T(8,128)S(1)}, u32[]{:S(2)}) copy-start(f32[76,80,128]{2,1,0:T(8,128)S(1)} %get-tuple-element.48.cy) | copy-start | bytes 9338884
  27.8 14.2 %copy-start.2 = (f32[76,80,128]{2,1,0:T(8,128)}, f32[76,80,128]{2,1,0:T(8,128)S(1)}, u32[]{:S(2)}) copy-start(f32[76,80,128]{2,1,0:T(8,128)S(1)} %get-tuple-element.49.cz) | copy-start | bytes 9338884
  27.8 14.2 %copy-start.4 = (f32[76,80,128]{2,1,0:T(8,128)}, f32[76,80,128]{2,1,0:T(8,128)S(1)}, u32[]{:S(2)}) copy-start(f32[76,80,128]{2,1,0:T(8,128)S(1)} %get-tuple-element.50.czm) | copy-start | bytes 9338884
  27.9 14.2 %collective-permute-start.4 = (f32[42,8,128]{2,1,0:T(8,128)S(1)}, f32[42,8,128]{2,1,0:T(8,128)S(1)}, u32[]{:S(2)}, u32[]{:S(2)}) collective-permute-start(f32[42,8,128]{2,1,0:T(8,128)S(1)} %get-tuple-element.54), channel_id=1, source_target_pairs={{0,1},{1,0},{2,3},{3,2},{4,5},{5,4},{6,7},{7,6},{8,9},{9,8},{10,11... | collective-permute-start | bytes 516104 | tf_op jit(solution)/shard_map/ppermute | solution.py:151
  30.8 11.3 %collective-permute-start.5 = (f32[42,8,128]{2,1,0:T(8,128)S(1)}, f32[42,8,128]{2,1,0:T(8,128)S(1)}, u32[]{:S(2)}, u32[]{:S(2)}) collective-permute-start(f32[42,8,128]{2,1,0:T(8,128)S(1)} %get-tuple-element.54), channel_id=1, source_target_pairs={{1,2},{2,1},{0,3},{3,0},{5,6},{6,5},{4,7},{7,4},{9,10},{10,9},{8,1... | collective-permute-start | bytes 516104 | tf_op jit(solution)/shard_map/ppermute | solution.py:155
  32.0 13.0 %copy-start.10 = (f32[32,64,256]{2,1,0:T(8,128)S(1)}, f32[32,64,256]{2,1,0:T(8,128)}, u32[]{:S(2)}) copy-start(f32[32,64,256]{2,1,0:T(8,128)} %measured.1) | copy-start | bytes 6291460
  32.0 13.1 %copy-start.11 = (s32[32,64,256]{2,1,0:T(8,128)S(1)}, s32[32,64,256]{2,1,0:T(8,128)}, u32[]{:S(2)}) copy-start(s32[32,64,256]{2,1,0:T(8,128)} %observed.1) | copy-start | bytes 6291460
  32.0 13.1 %copy-start.12 = (f32[32,64,256]{2,1,0:T(8,128)S(1)}, f32[32,64,256]{2,1,0:T(8,128)}, u32[]{:S(2)}) copy-start(f32[32,64,256]{2,1,0:T(8,128)} %adjoint.1) | copy-start | bytes 6291460
  45.1 16.5 %copy-start.5 = (f32[76,80,128]{2,1,0:T(8,128)S(1)}, f32[76,80,128]{2,1,0:T(8,128)}, u32[]{:S(2)}) copy-start(f32[76,80,128]{2,1,0:T(8,128)} %copy-done.4) | copy-start | bytes 9338884
  47.0 14.6 %copy-start.1 = (f32[76,80,128]{2,1,0:T(8,128)S(1)}, f32[76,80,128]{2,1,0:T(8,128)}, u32[]{:S(2)}) copy-start(f32[76,80,128]{2,1,0:T(8,128)} %copy-done) | copy-start | bytes 9338884
  47.0 9.9 %collective-permute-start.6 = (f32[8,64,128]{2,1,0:T(8,128)S(1)}, f32[8,64,128]{2,1,0:T(8,128)S(1)}, u32[]{:S(2)}, u32[]{:S(2)}) collective-permute-start(f32[8,64,128]{2,1,0:T(8,128)S(1)} %get-tuple-element.57), channel_id=1, source_target_pairs={{0,16},{16,0},{1,17},{17,1},{2,18},{18,2},{3,19},{19,3},{4,20},{20... | collective-permute-start | bytes 786440 | tf_op jit(solution)/shard_map/ppermute | solution.py:151
  47.4 4.3 %collective-permute-start.7 = (f32[32,8,128]{2,1,0:T(8,128)S(1)}, f32[32,8,128]{2,1,0:T(8,128)S(1)}, u32[]{:S(2)}, u32[]{:S(2)}) collective-permute-start(f32[32,8,128]{2,1,0:T(8,128)S(1)} %get-tuple-element.58), channel_id=1, source_target_pairs={{0,4},{4,0},{8,12},{12,8},{1,5},{5,1},{9,13},{13,9},{2,6},{6,2},{1... | collective-permute-start | bytes 393224 | tf_op jit(solution)/shard_map/ppermute | solution.py:151
  47.4 6.8 %collective-permute-start.8 = (f32[32,8,128]{2,1,0:T(8,128)S(1)}, f32[32,8,128]{2,1,0:T(8,128)S(1)}, u32[]{:S(2)}, u32[]{:S(2)}) collective-permute-start(f32[32,8,128]{2,1,0:T(8,128)S(1)} %get-tuple-element.59), channel_id=1, source_target_pairs={{4,8},{8,4},{0,0},{12,12},{5,9},{9,5},{1,1},{13,13},{6,10},{10,6},... | collective-permute-start | bytes 393224 | tf_op jit(solution)/shard_map/ppermute | solution.py:155
  54.2 2.8 %collective-permute-start.9 = (f32[8,8,128]{2,1,0:T(8,128)S(1)}, f32[8,8,128]{2,1,0:T(8,128)S(1)}, u32[]{:S(2)}, u32[]{:S(2)}) collective-permute-start(f32[8,8,128]{2,1,0:T(8,128)S(1)} %corner_kernel.3), channel_id=1, source_target_pairs={{0,16},{16,0},{1,17},{17,1},{2,18},{18,2},{3,19},{19,3},{4,20},{20... | collective-permute-start | bytes 98312 | tf_op jit(solution)/shard_map/ppermute | solution.py:151
  58.6 21.6 %collective-permute-start.10 = (f32[21,8,128]{2,1,0:T(8,128)S(1)}, f32[21,8,128]{2,1,0:T(8,128)S(1)}, u32[]{:S(2)}, u32[]{:S(2)}) collective-permute-start(f32[21,8,128]{2,1,0:T(8,128)S(1)} %get-tuple-element.69), channel_id=1, source_target_pairs={{0,1},{1,0},{2,3},{3,2},{4,5},{5,4},{6,7},{7,6},{8,9},{9,8},{10,11... | collective-permute-start | bytes 258056 | tf_op jit(solution)/shard_map/ppermute | solution.py:151
  61.4 18.8 %collective-permute-start.11 = (f32[21,8,128]{2,1,0:T(8,128)S(1)}, f32[21,8,128]{2,1,0:T(8,128)S(1)}, u32[]{:S(2)}, u32[]{:S(2)}) collective-permute-start(f32[21,8,128]{2,1,0:T(8,128)S(1)} %get-tuple-element.69), channel_id=1, source_target_pairs={{1,2},{2,1},{0,3},{3,0},{5,6},{6,5},{4,7},{7,4},{9,10},{10,9},{8,1... | collective-permute-start | bytes 258056 | tf_op jit(solution)/shard_map/ppermute | solution.py:155
  61.6 1.9 %copy-start.3 = (f32[76,80,128]{2,1,0:T(8,128)S(1)}, f32[76,80,128]{2,1,0:T(8,128)}, u32[]{:S(2)}) copy-start(f32[76,80,128]{2,1,0:T(8,128)} %copy-done.2) | copy-start | bytes 9338884
  80.2 3.5 %copy-start.7 = (s32[32,64,256]{2,1,0:T(8,128)S(1)}, s32[32,64,256]{2,1,0:T(8,128)}, u32[]{:S(2)}) copy-start(s32[32,64,256]{2,1,0:T(8,128)} %labels.3) | copy-start | bytes 6291460
  80.2 3.5 %copy-start.14 = (f32[4]{0:T(128)S(1)}, f32[4]{0:T(128)}, u32[]{:S(2)}) copy-start(f32[4]{0:T(128)} %scale.3) | copy-start | bytes 52
where the time goes:
time: 89.7 us; the launch traced here: 89.2 us
  Pallas kernels  49.6 us (55%)
  starting transfers between devices  18.1 us (20%)
  waiting for transfers between devices  13.4 us (15%)
  local copies, waits for them, and re-layouts  7.34 us (8%)
    pallas_call x9, Pallas kernels, call(): pl.pallas_call(functools.partial(kernel, plan), out_shape=tuple(outs), in...  49.6 us
    ppermute x4, starting transfers between devices, swap(): return (got, lax.ppermute(second, axis, pairs(count, True) + ends))  9.67 us
    ppermute x8, starting transfers between devices, swap(): got = lax.ppermute(first, axis, pairs(count, False))  8.39 us
    ppermute x8, waiting for transfers between devices, swap(): got = lax.ppermute(first, axis, pairs(count, False))  7.87 us
    unnamed x30, local copies, waits for them, and re-layouts  7.34 us
    ppermute x4, waiting for transfers between devices, swap(): return (got, lax.ppermute(second, axis, pairs(count, True) + ends))  5.52 us
  transfers between devices with their start and end apart: 12, of which 6 were waited for; matrix products, arithmetic and copies ran while one was open for 0% of the time, Pallas kernels for 30%

commit v1 on v0

--- a/solution.py
+++ b/solution.py
@@ -11,18 +11,18 @@
 MATERIALS = 4
 HALO = ITERS
 HALF_RATE = 0.5 * 0.15
-ROWS = 80
-OWN = 8
+OWN = HALO
 GROUPS = 4
 BLOCK = 128 // GROUPS
 F32 = jnp.float32
 
 in_vmem = pl.BlockSpec(memory_space=pltpu.VMEM)
 in_smem = pl.BlockSpec(memory_space=pltpu.SMEM)
-
-
-def params():
-    return pltpu.CompilerParams(vmem_limit_bytes=12 << 20)
+anywhere = pl.BlockSpec(memory_space=pl.ANY)
+
+
+def params(mib=3):
+    return pltpu.CompilerParams(vmem_limit_bytes=mib << 20)
 
 
 def vm(*shape):
@@ -54,6 +54,10 @@
 
 
 def load(ref, x, row, tiles):
+    if row < 0:
+        return [pltpu.roll(value, 1, axis=0) for value in load(ref, x, 0, tiles)]
+    if row + 8 > ref.shape[1]:
+        return [pltpu.roll(value, 7, axis=0) for value in load(ref, x, row - 1, tiles)]
     return [ref[x * tiles + t, pl.ds(row, 8), :] for t in range(tiles)]
 
 
@@ -87,6 +91,7 @@
         self.ny = shape[1] // self.sizes["gy"]
         self.nz = shape[2] // self.sizes["gz"]
         self.tiles = self.nz // 128
+        self.rows = self.ny + 2 * HALO
         self.two_sided = self.sizes["gx"] > 2
         self.deep = self.nx + HALO * (2 if self.two_sided else 1)
         self.planes = self.deep + 2
@@ -94,7 +99,7 @@
         self.edge_planes = self.per_group + 2
         self.row_tiles = [OWN - HALO + 8 * t for t in range((self.ny + 2 * HALO) // 8)]
         self.own_tiles = [OWN + 8 * t for t in range(self.ny // 8)]
-        self.unroll = 4 if self.two_sided else 3
+        self.end_tiles = [self.row_tiles[0], self.row_tiles[-1]]
         self.edge_vregs = self.per_group * len(self.row_tiles)
         self.face_vregs = -(-self.edge_vregs // 4)
 
@@ -115,15 +120,27 @@
             return jnp.int32(1 + HALO)
         return jnp.where(self.even("gx"), 1, 1 + HALO)
 
-    def span(self, step):
-        unroll = self.unroll
-        if step == ITERS - 1 and self.two_sided:
-            return self.own_plane(), self.nx
+    def core(self):
+        own = self.own_plane()
         if self.two_sided:
-            return 1, self.deep
-        need = self.nx + HALO - 1 - step
-        count = -(-need // unroll) * unroll
-        return jnp.where(self.even("gx"), 1, 1 + self.deep - count), count
+            return own + HALO, self.nx - 2 * HALO
+        return own + jnp.where(self.even("gx"), 0, HALO), self.nx - HALO
+
+    def beside(self, low, high, count):
+        own = self.own_plane()
+        if self.two_sided:
+            return [(own + low, count), (own + high, count)]
+        return [(own + jnp.where(self.even("gx"), high, low), count)]
+
+    def strips(self, step):
+        count = HALO - 1 - step
+        return self.beside(step + 1, self.nx - HALO, count) if count else []
+
+    def rims(self, step):
+        return self.beside(step + 1 - HALO, self.nx - HALO, 2 * HALO - 1 - step)
+
+    def masks(self):
+        return {row: self.row_keep(row) for row in self.row_tiles + self.own_tiles}
 
     def row_keep(self, row):
         if row < OWN:
@@ -188,7 +205,7 @@
     lax.fori_loop(0, plan.nx, body, 0, unroll=4)
 
 
-def corner_kernel(plan, per, ya, yb, out, out2):
+def corners(plan, per, ya, yb, out, out2=None):
     even = plan.even("gx")
     low, high = 0, (plan.nx - HALO) * per
     width = HALO * per
@@ -248,7 +265,7 @@
         half = HALO * per
         for j in range(HALO):
             put_rows(plane + j, c_ref.at[pl.ds(0, half)], c_ref.at[pl.ds(half, half)], j * per, blank)
-    zero = jnp.zeros((ROWS, 128), F32)
+    zero = jnp.zeros((plan.rows, 128), F32)
     for field in fields:
         for t in range(nt):
             field[t] = zero
@@ -331,25 +348,45 @@
     return values
 
 
-def face_coefficients(plan, k, cx, cy, cz, czm, planes, tiles):
-    def body(x, _):
-        for row in plan.row_tiles:
-            here = load(k, x, row, tiles)
-            store(cx, x, row, add(here, load(k, x + 1, row, tiles)))
-            store(cy, x, row, add(here, load(k, x, row + 1, tiles)))
-            store(cz, x, row, add(here, ahead(here)))
-            store(czm, x, row, add(here, behind(here)))
-        return 0
-
-    lax.fori_loop(0, planes - 1, body, 0, unroll=2)
-
-
-def step_forward(plan, v, w, c, start, count, unroll, row_tiles, tiles, keep, plane_keep):
+def face_coefficients(k, c, start, count, rows, tiles, unroll):
+    cx, cy, cz, czm = c
+
+    def body(i, _):
+        for j in range(unroll):
+            x = start + i * unroll + j
+            for row in rows:
+                here = load(k, x, row, tiles)
+                store(cx, x, row, add(here, load(k, x + 1, row, tiles)))
+                store(cy, x, row, add(here, load(k, x, row + 1, tiles)))
+                store(cz, x, row, add(here, ahead(here)))
+                store(czm, x, row, add(here, behind(here)))
+        return 0
+
+    repeat(body, count // unroll)
+
+
+def repeat(body, count):
+    if count == 1:
+        body(0, 0)
+    else:
+        lax.fori_loop(0, count, body, 0)
+
+
+def kept(total, mask, plane_keep, x):
+    if plane_keep is not None:
+        inside = plane_keep(x)
+        mask = inside if mask is None else mask & inside
+    if mask is None:
+        return total
+    return [jnp.where(mask, value, 0.0) for value in total]
+
+
+def step_forward(v, w, c, start, count, rows, tiles, masks, plane_keep, unroll):
     cx, cy, cz, czm = c
 
     def body(i, _):
         first = start + i * unroll
-        for row in row_tiles:
+        for row in rows:
             here = load(v, first, row, tiles)
             flow = mul(load(cx, first - 1, row, tiles), sub(here, load(v, first - 1, row, tiles)))
             for k in range(unroll):
@@ -364,31 +401,20 @@
                 right = mul(load(cz, x, row, tiles), sub(ahead(here), here))
                 left = mul(load(czm, x, row, tiles), sub(here, behind(here)))
                 total = add(total, sub(right, left))
-                store(w, x, row, kept(plan, total, row, keep, plane_keep, x))
+                store(w, x, row, kept(total, masks[row], plane_keep, x))
                 here = after
         return 0
 
-    lax.fori_loop(0, count // unroll, body, 0)
-
-
-def kept(plan, total, row, keep, plane_keep, x):
-    mask = plan.row_keep(row)
-    if keep is not None:
-        mask = keep if mask is None else mask & keep
-    if plane_keep is not None:
-        inside = plane_keep(x)
-        mask = inside if mask is None else mask & inside
-    if mask is None:
-        return total
-    return [jnp.where(mask, value, 0.0) for value in total]
-
-
-def step_backward(plan, v, w, u, acc, ay, az, c, start, count, unroll, row_tiles, tiles, keep, plane_keep, fresh):
+    repeat(body, count // unroll)
+
+
+def step_backward(v, w, u, sums, c, start, count, rows, tiles, masks, plane_keep, unroll, fresh):
     cx, cy, cz, czm = c
+    acc, az = sums
 
     def body(i, _):
         first = start + i * unroll
-        for row in row_tiles:
+        for row in rows:
             here = load(v, first, row, tiles)
             temp = load(u, first, row, tiles)
             diff = sub(here, load(v, first - 1, row, tiles))
@@ -404,24 +430,29 @@
                 term = mul(diff, sub(temp_after, temp))
                 both = add(part, term)
                 part = term
+                diff = sub(load(v, x, row + 1, tiles), here)
+                less = sub(here, load(v, x, row - 1, tiles))
+                up = mul(load(cy, x, row, tiles), diff)
+                down = mul(load(cy, x, row - 1, tiles), less)
+                total = add(total, sub(up, down))
+                both = add(both, mul(diff, sub(load(u, x, row + 1, tiles), temp)))
+                both = add(both, mul(less, sub(temp, load(u, x, row - 1, tiles))))
                 store(acc, x, row, both if fresh else add(both, load(acc, x, row, tiles)))
-                diff = sub(load(v, x, row + 1, tiles), here)
-                up = mul(load(cy, x, row, tiles), diff)
-                down = mul(load(cy, x, row - 1, tiles), sub(here, load(v, x, row - 1, tiles)))
-                total = add(total, sub(up, down))
-                term = mul(diff, sub(load(u, x, row + 1, tiles), temp))
-                store(ay, x, row, term if fresh else add(term, load(ay, x, row, tiles)))
                 diff = sub(ahead(here), here)
                 right = mul(load(cz, x, row, tiles), diff)
                 left = mul(load(czm, x, row, tiles), sub(here, behind(here)))
                 total = add(total, sub(right, left))
                 term = mul(diff, sub(ahead(temp), temp))
                 store(az, x, row, term if fresh else add(term, load(az, x, row, tiles)))
-                store(w, x, row, kept(plan, total, row, keep, plane_keep, x))
+                store(w, x, row, kept(total, masks[row], plane_keep, x))
                 here, temp = after, temp_after
         return 0
 
-    lax.fori_loop(0, count // unroll, body, 0)
+    repeat(body, count // unroll)
+
+
+def inner_unroll(count):
+    return next(n for n in (7, 6, 4, 2, 1) if count % n == 0)
 
 
 def plane_keeper(plan):
@@ -433,7 +464,7 @@
 
 
 def clear_ends(plan, fields):
-    zero = jnp.zeros((ROWS, 128), F32)
+    zero = jnp.zeros((plan.rows, 128), F32)
     nt = plan.tiles
     for field in fields:
         for t in range(nt):
@@ -441,10 +472,60 @@
             field[(plan.planes - 1) * nt + t] = zero
 
 
-def start_kernel(plan, scale, u0, diffusivity, labels, u, k, px, pya, pyb, *px2):
+def factor_of(labels, values):
+    out = jnp.zeros(labels.shape, F32) + values[0]
+    for m in range(1, MATERIALS):
+        out = jnp.where(labels == m, values[m], out)
+    return out
+
+
+def face_kernel(plan, scale, u0, diffusivity, labels, px, pya, pyb, *rest):
+    *px2, scale_s, ux, dx, lx, uy, dy, ly, sems = rest
+    nt, ny = plan.tiles, plan.ny
+    even_x, even_y = plan.even("gx"), plan.even("gy")
+    low, high = 0, plan.nx - HALO
+    starts = [jnp.where(even_x, high, low)] + ([jnp.where(even_x, low, high)] if plan.two_sided else [])
+    copies = [pltpu.make_async_copy(scale, scale_s, sems.at[0])]
+    for s, at in enumerate(starts):
+        for n, (source, held) in enumerate(((u0, ux), (diffusivity, dx), (labels, lx))):
+            copies.append(pltpu.make_async_copy(source.at[pl.ds(at, HALO)], held.at[s], sems.at[1 + 3 * s + n]))
+    for s, at in enumerate((0, ny - 8)):
+        for n, (source, held) in enumerate(((u0, uy), (diffusivity, dy), (labels, ly))):
+            copies.append(
+                pltpu.make_async_copy(source.at[:, pl.ds(at, 8), :], held.at[s], sems.at[7 + 3 * s + n])
+            )
+    for copy in copies:
+        copy.start()
+    for copy in copies:
+        copy.wait()
+    values = [scale_s[m] for m in range(MATERIALS)]
+    wide = HALO * nt
+    for s, out in enumerate((px, *px2)):
+        for j in range(HALO):
+            for t in range(nt):
+                cols = pl.ds(128 * t, 128)
+                out[j * nt + t] = ux[s, j, :, cols]
+                out[wide + j * nt + t] = dx[s, j, :, cols] * factor_of(lx[s, j, :, cols], values) * HALF_RATE
+
+    def body(x, _):
+        for t in range(nt):
+            cols = pl.ds(128 * t, 128)
+            k = [dy[s, x, :, cols] * factor_of(ly[s, x, :, cols], values) * HALF_RATE for s in range(2)]
+            u = [uy[s, x, :, cols] for s in range(2)]
+            for f, (a, b) in enumerate((u, k)):
+                a, b = a[:HALO], b[8 - HALO :]
+                pya[x * nt + t, pl.ds(HALO * f, HALO), :] = jnp.where(even_y, b, a)
+                pyb[x * nt + t, pl.ds(HALO * f, HALO), :] = jnp.where(even_y, a, b)
+        return 0
+
+    lax.fori_loop(0, plan.nx, body, 0, unroll=4)
+
+
+def own_kernel(plan, scale, u0, diffusivity, labels, u, k, cx, cy, cz, czm):
     nt = plan.tiles
     own = plan.own_plane()
     values = [scale[m] for m in range(MATERIALS)]
+    clear_ends(plan, (u, k))
 
     def body(x, _):
         for t in range(nt):
@@ -456,57 +537,69 @@
         return 0
 
     lax.fori_loop(0, plan.nx, body, 0, unroll=2)
-    send_faces(plan, (u, k), px, px2[0] if px2 else None, pya, pyb)
-
-
-def factor_of(labels, values):
-    out = jnp.zeros(labels.shape, F32) + values[0]
-    for m in range(1, MATERIALS):
-        out = jnp.where(labels == m, values[m], out)
-    return out
-
-
-def ready_kernel(plan, u, k, xa, xb, ya, yb, ca, cb, u_out, k_out, cx, cy, cz, czm, eu, ek, pz):
-    del u, k
-    place_halos(plan, (u_out, k_out), xa, xb, ya, yb, ca, cb)
-    face_coefficients(plan, k_out, cx, cy, cz, czm, plan.planes, plan.tiles)
-    pack_edges(plan, u_out, eu, plan.row_tiles)
-    pack_edges(plan, k_out, ek, plan.row_tiles)
+    face_coefficients(k, (cx, cy, cz, czm), own - 1, plan.nx + 1, plan.own_tiles, nt, 3)
+
+
+def inner_forward_kernel(plan, steps, sources, *refs):
+    c, fields = refs[:4], refs[4:]
+    clear_ends(plan, fields[sources:])
+    masks = dict.fromkeys(plan.own_tiles)
+    start, count = plan.core()
+    for n, step in enumerate(steps):
+        v, w = fields[sources - 1 + n], fields[sources + n]
+        step_forward(v, w, c, start, count, plan.own_tiles, plan.tiles, masks, None, inner_unroll(count))
+        for at, many in plan.strips(step):
+            step_forward(v, w, c, at, many, plan.own_tiles, plan.tiles, masks, None, many)
+
+
+def ready_kernel(plan, xa, xb, ya, yb, ca, cb, u_in, k_in, u, k, eu, ek, pz):
+    del u_in, k_in
+    place_halos(plan, (u, k), xa, xb, ya, yb, ca, cb)
+    pack_edges(plan, u, eu, plan.row_tiles)
+    pack_edges(plan, k, ek, plan.row_tiles)
     pack_faces(plan, eu, pz, 0)
     pack_faces(plan, ek, pz, plan.face_vregs)
 
 
-def forward_kernel(plan, u0, cx, cy, cz, czm, u1, u2, u3, u4):
-    fields = (u0, u1, u2, u3, u4)
-    clear_ends(plan, fields[1:ITERS])
-    keeper = plane_keeper(plan)
+def outer_forward_kernel(plan, u, k, *refs):
+    c, later = refs[8:12], refs[12:]
+    nt = plan.tiles
+    own = plan.own_plane()
+    face_coefficients(k, c, own - 1, plan.nx + 1, plan.end_tiles, nt, 11)
+    for at, many in plan.beside(-HALO - 1, plan.nx - HALO - 1, 2 * HALO + 1):
+        face_coefficients(k, c, at, many, plan.row_tiles, nt, 3)
+    fields = (u, *later)
+    masks, keeper = plan.masks(), plane_keeper(plan)
+    start, count = plan.core()
     for n in range(ITERS):
-        start, count = plan.span(n)
-        tiles = plan.own_tiles if n == ITERS - 1 else plan.row_tiles
-        step_forward(plan, fields[n], fields[n + 1], (cx, cy, cz, czm), start, count, plan.unroll, tiles, plan.tiles, None, keeper)
-
-
-def edge_forward_kernel(plan, eu, ek, za, zb, e0, u1, u2, u3, u4, cx, cy, cz, czm, k):
-    e0[...] = eu[...]
-    k[...] = ek[...]
+        step_forward(fields[n], fields[n + 1], c, start, count, plan.end_tiles, nt, masks, None, 2 * inner_unroll(count))
+        for at, many in plan.rims(n):
+            step_forward(fields[n], fields[n + 1], c, at, many, plan.row_tiles, nt, masks, keeper, many)
+
+
+def edge_masks(plan):
+    keep = plan.edge_keep()
+    return {row: keep if mask is None else keep & mask for row, mask in plan.masks().items()}
+
+
+def edge_forward_kernel(plan, eu, k_in, za, zb, e0, k, u1, u2, u3, u4, cx, cy, cz, czm):
+    del eu, k_in
     place_faces(plan, e0, za, zb, 0)
     place_faces(plan, k, za, zb, plan.face_vregs)
     wrap_planes(plan, e0)
     wrap_planes(plan, k)
-    face_coefficients(plan, k, cx, cy, cz, czm, plan.edge_planes, 1)
-    keep = plan.edge_keep()
-    keeper = edge_keeper(plan)
+    c = (cx, cy, cz, czm)
+    face_coefficients(k, c, 0, plan.per_group + 1, plan.row_tiles, 1, plan.per_group + 1)
+    masks, keeper = edge_masks(plan), edge_keeper(plan)
     fields = (e0, u1, u2, u3, u4)
     for n in range(ITERS):
-        step_forward(plan, fields[n], fields[n + 1], (cx, cy, cz, czm), 1, plan.per_group, edge_unroll(plan), plan.row_tiles, 1, keep, keeper)
+        step_forward(fields[n], fields[n + 1], c, 1, plan.per_group, plan.row_tiles, 1, masks, keeper, plan.per_group)
         wrap_planes(plan, fields[n + 1])
 
 
-def edge_unroll(plan):
-    return 3 if plan.per_group % 3 == 0 else 2
-
-
 def edge_keeper(plan):
+    if not plan.two_sided:
+        return None
     group = lanes() // BLOCK
     low = jnp.where(plan.first("gx"), plan.own_plane(), 1)
     high = jnp.where(plan.last("gx"), plan.own_plane() + plan.nx, plan.planes)
@@ -515,7 +608,7 @@
         plane = group * plan.per_group + i
         return (plane >= low) & (plane < high)
 
-    return inside if plan.two_sided else None
+    return inside
 
 
 def middle_kernel(plan, u4, e4, measured, observed, adjoint, lam, px, pya, pyb, *px2):
@@ -531,162 +624,237 @@
             store(lam, own + x, row, temp)
         return 0
 
-    lax.fori_loop(0, plan.nx, body, 0, unroll=2)
+    lax.fori_loop(0, plan.nx, body, 0, unroll=4)
+    clear_ends(plan, (lam,))
     send_faces(plan, (lam,), px, px2[0] if px2 else None, pya, pyb)
 
 
-def turn_kernel(plan, lam, xa, xb, ya, yb, ca, cb, lam_out, edge, pz):
-    del lam
-    place_halos(plan, (lam_out,), xa, xb, ya, yb, ca, cb)
-    pack_edges(plan, lam_out, edge, plan.row_tiles)
+def inner_backward_kernel(plan, steps, fresh, given, *refs):
+    c, temps = refs[:4], refs[4 : 4 + len(steps)]
+    rest = refs[4 + len(steps) + given :]
+    lams, sums = refs[4 + len(steps) : 5 + len(steps)] + rest[: len(steps)], rest[len(steps) :]
+    clear_ends(plan, lams[1:])
+    masks = dict.fromkeys(plan.own_tiles)
+    start, count = plan.core()
+    for n, step in enumerate(steps):
+        v, w = lams[n], lams[n + 1]
+        step_backward(
+            v, w, temps[n], sums, c, start, count, plan.own_tiles, plan.tiles, masks, None,
+            inner_unroll(count), fresh and n == 0,
+        )
+        for at, many in plan.strips(step):
+            step_forward(v, w, c, at, many, plan.own_tiles, plan.tiles, masks, None, many)
+
+
+def turn_kernel(plan, xa, xb, ya, yb, ca, cb, lam_in, lam, edge, pz):
+    del lam_in
+    place_halos(plan, (lam,), xa, xb, ya, yb, ca, cb)
+    pack_edges(plan, lam, edge, plan.row_tiles)
     pack_faces(plan, edge, pz, 0)
 
 
-def backward_kernel(plan, lam, u0, u1, u2, u3, cx, cy, cz, czm, w, other, acc, ay, az):
-    fields = (u0, u1, u2, u3)
-    clear_ends(plan, (w, other))
-    keeper = plane_keeper(plan)
+def outer_backward_kernel(plan, lam, *refs):
+    c, temps, rest = refs[:4], refs[4:8], refs[14:]
+    later, sums = rest[:4], rest[4:]
     nt = plan.tiles
-    buffers = [lam, other, w, other, w]
+    fields = (lam, *later)
+    masks, keeper = plan.masks(), plane_keeper(plan)
+    start, count = plan.core()
     for m in range(ITERS):
-        start, count = plan.span(m)
-        tiles = plan.own_tiles if m == ITERS - 1 else plan.row_tiles
-        n = ITERS - 1 - m
+        v, w, u = fields[m], fields[m + 1], temps[ITERS - 1 - m]
         step_backward(
-            plan, buffers[m], buffers[m + 1], fields[n], acc, ay, az, (cx, cy, cz, czm),
-            start, count, plan.unroll, tiles, nt, None, keeper, m == 0,
+            v, w, u, sums, c, start, count, plan.end_tiles, nt, masks, None, 2 * inner_unroll(count), m == 0
         )
-    own = plan.own_plane()
-
-    def body(x, _):
-        at, row = own + x, OWN - 8
-        v, u = buffers[ITERS - 1], fields[0]
-        term = mul(
-            sub(load(v, at, row + 1, nt), load(v, at, row, nt)),
-            sub(load(u, at, row + 1, nt), load(u, at, row, nt)),
-        )
-        for t in range(nt):
-            ay[at * nt + t, pl.ds(OWN - 1, 1), :] += term[t][7:8]
-        return 0
-
-    lax.fori_loop(0, plan.nx, body, 0, unroll=4)
-
-
-def edge_backward_kernel(plan, lam, za, zb, u0, u1, u2, u3, cx, cy, cz, czm, w, total, e, other, acc, ay, az):
+        for at, many in plan.rims(m):
+            step_backward(v, w, u, sums, c, at, many, plan.row_tiles, nt, masks, keeper, many, m == 0)
+
+
+def edge_backward_kernel(plan, lam, za, zb, u0, u1, u2, u3, cx, cy, cz, czm, w, total, e, other, acc, az):
     e[...] = lam[...]
     place_faces(plan, e, za, zb, 0)
     wrap_planes(plan, e)
-    keep = plan.edge_keep()
-    keeper = edge_keeper(plan)
+    masks, keeper = edge_masks(plan), edge_keeper(plan)
     fields = (u0, u1, u2, u3)
     buffers = [e, other, w, other, w]
     for m in range(ITERS):
         n = ITERS - 1 - m
         step_backward(
-            plan, buffers[m], buffers[m + 1], fields[n], acc, ay, az, (cx, cy, cz, czm),
-            1, plan.per_group, edge_unroll(plan), plan.row_tiles, 1, keep, keeper, m == 0,
+            buffers[m], buffers[m + 1], fields[n], (acc, az), (cx, cy, cz, czm),
+            1, plan.per_group, plan.row_tiles, 1, masks, keeper, plan.per_group, m == 0,
         )
         if m < ITERS - 1:
             wrap_planes(plan, buffers[m + 1])
-
-    def body(i, _):
+    for i in range(1, 1 + plan.per_group):
         for row in plan.own_tiles:
-            z = [az[i + 1, pl.ds(row, 8), :]]
-            whole = acc[i + 1, pl.ds(row, 8), :] + ay[i + 1, pl.ds(row, 8), :] + ay[i + 1, pl.ds(row - 1, 8), :]
-            total[i + 1, pl.ds(row, 8), :] = whole + z[0] + behind(z)[0]
-        return 0
-
-    lax.fori_loop(0, plan.per_group, body, 0)
-
-
-def finish_kernel(plan, scale, labels, lam, acc, ay, az, e_lam, e_total, gradient, adjoint):
+            z = [az[i, pl.ds(row, 8), :]]
+            total[i, pl.ds(row, 8), :] = acc[i, pl.ds(row, 8), :] + z[0] + behind(z)[0]
+
+
+def finish_kernel(plan, scale, labels, lam, acc, az, e_lam, e_total, gradient, adjoint, grad_s, adj_s, sems):
     nt = plan.tiles
     own = plan.own_plane()
     values = [scale[m] for m in range(MATERIALS)]
-
-    def body(x, _):
-        p = own + x
-        for row in plan.own_tiles:
-            z = load(az, p, row, nt)
-            total = add(load(acc, p, row, nt), add(load(ay, p, row, nt), load(ay, p, row - 1, nt)))
-            total = add(total, add(z, behind(z)))
-            total = merge_edges(plan, total, e_total, p, row)
-            end = merge_edges(plan, load(lam, p, row, nt), e_lam, p, row)
-            for t in range(nt):
-                at = (x, pl.ds(row - OWN, 8), pl.ds(128 * t, 128))
-                gradient[at] = total[t] * (-HALF_RATE) * factor_of(labels[at], values)
-                adjoint[at] = end[t]
-        return 0
-
-    lax.fori_loop(0, plan.nx, body, 0, unroll=2)
-
-
-def call(kernel, plan, outs, args, alias=None, scratch=(), smem=0, flops=0):
-    specs = [in_smem] * smem + [in_vmem] * (len(args) - smem)
+    chunk = 4
+
+    def copies(i):
+        at = pl.ds(i * chunk, chunk)
+        return (
+            pltpu.make_async_copy(grad_s.at[at], gradient.at[at], sems.at[0, i]),
+            pltpu.make_async_copy(adj_s.at[at], adjoint.at[at], sems.at[1, i]),
+        )
+
+    def body(i, _):
+        for j in range(chunk):
+            x = i * chunk + j
+            p = own + x
+            for row in plan.own_tiles:
+                z = load(az, p, row, nt)
+                total = add(load(acc, p, row, nt), add(z, behind(z)))
+                total = merge_edges(plan, total, e_total, p, row)
+                end = merge_edges(plan, load(lam, p, row, nt), e_lam, p, row)
+                for t in range(nt):
+                    at = (x, pl.ds(row - OWN, 8), pl.ds(128 * t, 128))
+                    grad_s[at] = total[t] * (-HALF_RATE) * factor_of(labels[at], values)
+                    adj_s[at] = end[t]
+        for copy in copies(i):
+            copy.start()
+        return 0
+
+    lax.fori_loop(0, plan.nx // chunk, body, 0)
+
+    def drain(i, _):
+        for copy in copies(i):
+            copy.wait()
+        return 0
+
+    lax.fori_loop(0, plan.nx // chunk, drain, 0)
+
+
+def call(kernel, outs, args, alias=None, scratch=(), smem=0, flops=0, specs=None, out_spec=in_vmem, mib=3):
+    if specs is None:
+        specs = [in_smem] * smem + [in_vmem] * (len(args) - smem)
     cost = pl.CostEstimate(flops=flops, bytes_accessed=flops, transcendentals=0) if flops else None
     return pl.pallas_call(
-        functools.partial(kernel, plan),
+        kernel,
         out_shape=tuple(outs),
         in_specs=specs,
-        out_specs=(in_vmem,) * len(outs),
+        out_specs=(out_spec,) * len(outs),
         input_output_aliases=alias or {},
         scratch_shapes=list(scratch),
         cost_estimate=cost,
-        compiler_params=params(),
-        name=kernel.__name__,
+        compiler_params=params(mib),
+        name=kernel.func.__name__,
     )(*args)
 
 
 def shards(plan, checkpoint, diffusivity, material_scale, labels, measured, observed, adjoint_in):
-    nt = plan.tiles
-    work = vm(plan.planes * nt, ROWS, 128)
-    edge = vm(plan.edge_planes, ROWS, 128)
-    wide = HALO * nt
+    nt, nx, ny, nz = plan.tiles, plan.nx, plan.ny, plan.nz
+    part = functools.partial
+    work = vm(plan.planes * nt, plan.rows, 128)
+    edge = vm(plan.edge_planes, plan.rows, 128)
+    sides = 2 if plan.two_sided else 1
 
     def faces(count):
-        x = vm(count * wide, plan.ny, 128)
-        y = vm(plan.nx * nt * count // 2, 2 * HALO, 128)
-        return (x, y, y) + ((x,) if plan.two_sided else ())
-
-    def exchange(count, sent):
+        x = vm(count * HALO * nt, ny, 128)
+        y = vm(nx * nt * count // 2, 2 * HALO, 128)
+        return (x, y, y) + (x,) * (sides - 1)
+
+    def exchange(count, sent, between):
         px, pya, pyb = sent[:3]
-        px2 = sent[3] if plan.two_sided else None
-        xa, xb = swap(plan, "gx", px, px2, False)
+        xa, xb = swap(plan, "gx", px, sent[-1], False)
         ya, yb = swap(plan, "gy", pya, pyb, False)
         per = nt * count // 2
         corner = vm(2 * HALO * per, 2 * HALO, 128)
-        body = functools.partial(corner_kernel, plan, per)
-        if plan.two_sided:
-            shapes, fn = (corner, corner), body
-        else:
-            shapes, fn = (corner,), lambda ya, yb, out: body(ya, yb, out, None)
-        corners = pl.pallas_call(
-            fn, out_shape=shapes, in_specs=[in_vmem] * 2, out_specs=(in_vmem,) * len(shapes),
-            compiler_params=params(), name="corner_kernel",
-        )(ya, yb)
-        ca, cb = swap(plan, "gx", corners[0], corners[-1], False)
-        return xa, xb, ya, yb, ca, cb
-
-    u, k, *sent = call(start_kernel, plan, (work, work) + faces(2), (material_scale, checkpoint, diffusivity, labels), smem=1)
-    got = exchange(2, sent)
-    u, k, cx, cy, cz, czm, eu, ek, pz = call(
-        ready_kernel, plan, (work, work, work, work, work, work, edge, edge, vm(2 * plan.face_vregs, 8, 128)),
-        (u, k) + got, alias={0: 0, 1: 1},
-    )
-    c = (cx, cy, cz, czm)
+
+        def corner_kernel(ya, yb, _, *out):
+            corners(plan, per, ya, yb, *out)
+
+        got = call(part(corner_kernel), (corner,) * sides, (ya, yb, between()))
+        ca, cb = swap(plan, "gx", got[0], got[-1], False)
+        return (xa, xb, ya, yb, ca, cb), got[0]
+
+    hbm = [pltpu.with_memory_space_constraint(a, pltpu.HBM) for a in (material_scale, checkpoint, diffusivity, labels)]
+    held = [vm(sides, HALO, ny, nz)] * 2 + [pltpu.VMEM((sides, HALO, ny, nz), jnp.int32)]
+    held += [vm(2, nx, 8, nz)] * 2 + [pltpu.VMEM((2, nx, 8, nz), jnp.int32)]
+    sent = call(
+        part(face_kernel, plan), faces(2), hbm, specs=[anywhere] * 4, mib=8,
+        scratch=[pltpu.SMEM((MATERIALS,), F32), *held, pltpu.SemaphoreType.DMA((13,))],
+    )
+    u, k, *c = call(part(own_kernel, plan), (work,) * 6, (material_scale, checkpoint, diffusivity, labels), smem=1, flops=1 << 23)
+    state = {}
+
+    def first_half():
+        state["c"], state["u"], state["new"] = c, u, call(
+            part(lambda *refs: inner_forward_kernel(plan, (0, 1), 1, *refs)), (work,) * 2, (*c, u), flops=1 << 23
+        )
+        return state["new"][0]
+
+    got, mark = exchange(2, sent, first_half)
+    u1, u2 = state["new"]
+
+    def later_half(mark, *refs):
+        del mark
+        inner_forward_kernel(plan, (2, 3), 1, *refs)
+
+    u3, u4 = call(part(later_half), (work,) * 2, (mark, *c, u2), flops=1 << 23)
+    u, k, eu, ek, pz = call(
+        part(after(ready_kernel), plan), (work, work, edge, edge, vm(2 * plan.face_vregs, 8, 128)),
+        (u4, *got, u, k), alias={7: 0, 8: 1},
+    )
     za, zb = swap(plan, "gz", pz, pz, True)
-    u1, u2, u3, u4 = call(forward_kernel, plan, (work,) * 4, (u,) + c, flops=1 << 24)
-    e0, e1, e2, e3, e4, ex, ey, ez, ezm = call(edge_forward_kernel, plan, (edge,) * 9, (eu, ek, za, zb), scratch=(edge,))
-    lam, *sent = call(middle_kernel, plan, (work,) + faces(1), (u4, e4, measured, observed, adjoint_in))
-    got = exchange(1, sent)
-    lam, e_lam, pz = call(turn_kernel, plan, (work, edge, vm(plan.face_vregs, 8, 128)), (lam,) + got, alias={0: 0})
+    out = call(
+        part(outer_forward_kernel, plan), (work,) * 8, (u, k, *c, u1, u2, u3, u4),
+        alias={2 + i: i for i in range(8)}, flops=1 << 24,
+    )
+    c, (u1, u2, u3, u4) = out[:4], out[4:]
+    e0, _, e1, e2, e3, e4, ex, ey, ez, ezm = call(
+        part(edge_forward_kernel, plan), (edge,) * 10, (eu, ek, za, zb), alias={0: 0, 1: 1}
+    )
+    lam, *sent = call(
+        part(middle_kernel, plan), (work,) + faces(1), (u4, e4, measured, observed, adjoint_in), alias={0: 0}
+    )
+
+    def first_back():
+        state["new"] = call(
+            part(lambda *refs: inner_backward_kernel(plan, (0, 1), True, 1, *refs)), (work,) * 4,
+            (*c, u3, u2, lam), flops=1 << 24,
+        )
+        return state["new"][0]
+
+    got, mark = exchange(1, sent, first_back)
+    l3, l2, acc, az = state["new"]
+
+    def later_back(mark, *refs):
+        del mark
+        inner_backward_kernel(plan, (2, 3), False, 3, *refs)
+
+    l1, l0, acc, az = call(
+        part(later_back), (work,) * 4, (mark, *c, u1, u, l2, acc, az), alias={8: 2, 9: 3}, flops=1 << 24
+    )
+    lam, e_lam, pz = call(
+        part(after(turn_kernel), plan), (work, edge, vm(plan.face_vregs, 8, 128)), (l0, *got, lam), alias={7: 0}
+    )
     za, zb = swap(plan, "gz", pz, pz, True)
-    start, _, acc, ay, az = call(backward_kernel, plan, (work,) * 5, (lam, u, u1, u2, u3) + c, flops=1 << 25)
+    l3, l2, l1, l0, acc, az = call(
+        part(outer_backward_kernel, plan), (work,) * 6, (lam, *c, u, u1, u2, u3, l3, l2, l1, l0, acc, az),
+        alias={9 + i: i for i in range(6)}, flops=1 << 25,
+    )
     e_start, e_total = call(
-        edge_backward_kernel, plan, (edge,) * 2, (e_lam, za, zb, e0, e1, e2, e3, ex, ey, ez, ezm), scratch=(edge,) * 5
-    )
-    block = jax.ShapeDtypeStruct((plan.nx, plan.ny, plan.nz), F32)
-    return call(finish_kernel, plan, (block, block), (material_scale, labels, start, acc, ay, az, e_start, e_total), smem=1)
+        part(edge_backward_kernel, plan), (edge,) * 2, (e_lam, za, zb, e0, e1, e2, e3, ex, ey, ez, ezm), scratch=(edge,) * 4
+    )
+    block = jax.ShapeDtypeStruct((nx, ny, nz), F32)
+    return call(
+        part(finish_kernel, plan), (block, block), (material_scale, labels, l0, acc, az, e_start, e_total), smem=1,
+        out_spec=anywhere, mib=6, scratch=[vm(nx, ny, nz), vm(nx, ny, nz), pltpu.SemaphoreType.DMA((2, nx // 4))],
+    )
+
+
+def after(kernel):
+    @functools.wraps(kernel)
+    def waiting(plan, _, *refs):
+        kernel(plan, *refs)
+
+    return waiting
 
 
 def solution(mesh):

time: 89.7 us -> 66.9 us (0.75)
  waiting for transfers between devices: 13.4 us -> 1.09 us
  local copies, waits for them, and re-layouts: 7.34 us -> 1.56 us
  Pallas kernels: 49.6 us -> 45.8 us
  starting transfers between devices: 18.1 us -> 16.8 us
    ppermute x8, waiting for transfers between devices: 7.87 us -> 0.09 us  [swap(): got = lax.ppermute(first, axis, pairs(count, False))]
    unnamed x30 -> x22, local copies, waits for them, and re-layouts: 7.34 us -> 1.56 us
    ppermute x4, waiting for transfers between devices: 5.52 us -> 1 us  [swap(): return (got, lax.ppermute(second, axis, pairs(count, True) + ends))]
    pallas_call x11 -> x16, Pallas kernels: 49.6 us -> 45.8 us  [call(): pl.pallas_call(kernel, out_shape=tuple(outs), in_specs=specs, out_specs=(...]
    ppermute x8, starting transfers between devices: 8.39 us -> 6.59 us  [swap(): got = lax.ppermute(first, axis, pairs(count, False))]
  transfers between devices with their start and end apart: 12 -> 12, of which waited for: 6 -> 2; matrix products, arithmetic and copies ran while one was open for 0% -> 0% of each run, Pallas kernels for 30% -> 43%
where the time goes in v1:
time: 66.9 us; the launch traced here: 66.3 us
  Pallas kernels  45.8 us (68%)
  starting transfers between devices  16.8 us (25%)
  local copies, waits for them, and re-layouts  1.56 us (2%)
  between operations  1.11 us (2%)
  waiting for transfers between devices  1.09 us (2%)
    pallas_call x16, Pallas kernels, call(): pl.pallas_call(kernel, out_shape=tuple(outs), in_specs=specs, out_specs=(...  45.8 us
    ppermute x4, starting transfers between devices, swap(): return (got, lax.ppermute(second, axis, pairs(count, True) + ends))  10.2 us
    ppermute x8, starting transfers between devices, swap(): got = lax.ppermute(first, axis, pairs(count, False))  6.59 us
    unnamed x22, local copies, waits for them, and re-layouts  1.56 us
  transfers between devices with their start and end apart: 12, of which 2 were waited for; matrix products, arithmetic and copies ran while one was open for 0% of the time, Pallas kernels for 43%

profile of v1, /device:TPU:9, one launch (start us, length us, event | category | flops | bytes accessed | tf_op | source)
XLA Modules:
  0.0 66.3 jit_solution(8870678526125163745)
XLA Ops:
  0.6 0.0 copy-start.4
  0.6 0.0 copy-start.5
  0.7 0.0 copy-start.6
  0.7 0.0 copy-start.10
  0.7 2.2 %face_kernel.1 = (f32[16,64,128]{2,1,0:T(8,128)S(1)}, f32[64,8,128]{2,1,0:T(8,128)S(1)}, f32[64,8,128]{2,1,0:T(8,128)S(1)}) custom-call(f32[4]{0:T(128)} %scale.5, f32[32,64,256]{2,1,0:T(8,128)} %u0.3, f32[32,64,256]{2,1,0:T(8,128)} %diffusivity.3, s32[32,64,256]{2,1,0:T(8,128)} %labels.5), custom_call_target="tpu_custom_call" | custom-call | tf_op jit(solution)/shard_map/face_kernel/pallas_call | solution.py:737
  2.9 1.3 %collective-permute-start.2 = (f32[16,64,128]{2,1,0:T(8,128)S(1)}, f32[16,64,128]{2,1,0:T(8,128)S(1)}, u32[]{:S(2)}, u32[]{:S(2)}) collective-permute-start(f32[16,64,128]{2,1,0:T(8,128)S(1)} %get-tuple-element.67), channel_id=1, source_target_pairs={{0,16},{16,0},{1,17},{17,1},{2,18},{18,2},{3,19},{19,3},{4,20},{20... | collective-permute-start | bytes 1572872 | tf_op jit(solution)/shard_map/ppermute | solution.py:168
  4.1 0.2 collective-permute-start
  4.3 4.3 %collective-permute-start.1 = (f32[64,8,128]{2,1,0:T(8,128)S(1)}, f32[64,8,128]{2,1,0:T(8,128)S(1)}, u32[]{:S(2)}, u32[]{:S(2)}) collective-permute-start(f32[64,8,128]{2,1,0:T(8,128)S(1)} %get-tuple-element.58), channel_id=1, source_target_pairs={{4,8},{8,4},{0,0},{12,12},{5,9},{9,5},{1,1},{13,13},{6,10},{10,6},... | collective-permute-start | bytes 786440 | tf_op jit(solution)/shard_map/ppermute | solution.py:172
  8.6 0.0 copy-done.4
  8.7 0.0 copy-done.5
  8.7 0.0 copy-done.6
  8.7 0.0 copy-done.10
  8.7 3.2 %own_kernel.1 = (f32[76,72,128]{2,1,0:T(8,128)S(1)}, f32[76,72,128]{2,1,0:T(8,128)S(1)}, f32[76,72,128]{2,1,0:T(8,128)S(1)}, f32[76,72,128]{2,1,0:T(8,128)S(1)},...) custom-call(f32[4]{0:T(128)S(1)} %copy-done.10, f32[32,64,256]{2,1,0:T(8,128)S(1)} %copy-done.5, ...), custom_call_target="tpu_custom_call" | custom-call | flops 8388608 | bytes 8388608 | tf_op jit(solution)/shard_map/own_kernel/pallas_call | solution.py:737
  11.9 3.0 %_lambda_.2 = (f32[76,72,128]{2,1,0:T(8,128)S(1)}, f32[76,72,128]{2,1,0:T(8,128)S(1)}) custom-call(f32[76,72,128]{2,1,0:T(8,128)S(1)} %get-tuple-element.59.refs_0_, f32[76,72,128]{2,1,0:T(8,128)S(1)} %get-tuple-element.60.refs_1_, f32[76,72,128]{2,1,0:T(8,128)S(1)} %get-tuple-element.61.refs_2_, f32[76,72,128]{2,1,0:T(8,128)S(1)} %get-tuple-element.62.refs_3_, ...), custom_call_target="tpu_custom_call" | custom-call | flops 8388608 | bytes 8388608 | tf_op jit(solution)/shard_map/<lambda>/pallas_call | solution.py:737
  14.9 0.0 collective-permute-done.ya.args_3_
  14.9 0.0 collective-permute-done.1.yb.args_4_
  15.0 0.3 collective-permute-start.3
  15.3 2.8 %later_half.1 = (f32[76,72,128]{2,1,0:T(8,128)S(1)}, f32[76,72,128]{2,1,0:T(8,128)S(1)}) custom-call(f32[16,8,128]{2,1,0:T(8,128)S(1)} %corner_kernel.2.mark, f32[76,72,128]{2,1,0:T(8,128)S(1)} %get-tuple-element.59.refs_0_, f32[76,72,128]{2,1,0:T(8,128)S(1)} %get-tuple-element.60.refs_1_, f32[76,72,128]{2,1,0:T(8,128)S(1)} %get-tuple-element.61.refs_2_, ...), custom_call_target="tpu_custom_call" | custom-call | flops 8388608 | bytes 8388608 | tf_op jit(solution)/shard_map/later_half/pallas_call | solution.py:737
  18.1 0.1 collective-permute-done.3.args_5_.args_6_
  18.1 0.0 collective-permute-done.2.args_1_.args_2_
  18.1 3.2 %ready_kernel.1 = (f32[76,72,128]{2,1,0:T(8,128)S(1)}, f32[76,72,128]{2,1,0:T(8,128)S(1)}, f32[11,72,128]{2,1,0:T(8,128)S(1)}, f32[11,72,128]{2,1,0:T(8,128)S(1)}, f32[42,8,128]{2,1,0:T(8,128)S(1)}) custom-call(f32[76,72,128]{2,1,0:T(8,128)S(1)} %get-tuple-element.66.args_0_.refs_7_, ...), custom_call_target="tpu_custom_call", output_to_operand_aliasing={{0}: (7, {}), {1}: (8, {})} | custom-call | tf_op jit(solution)/shard_map/ready_kernel/pallas_call | solution.py:737
  21.3 2.7 %collective-permute-start.4 = (f32[42,8,128]{2,1,0:T(8,128)S(1)}, f32[42,8,128]{2,1,0:T(8,128)S(1)}, u32[]{:S(2)}, u32[]{:S(2)}) collective-permute-start(f32[42,8,128]{2,1,0:T(8,128)S(1)} %get-tuple-element.75), channel_id=1, source_target_pairs={{0,1},{1,0},{2,3},{3,2},{4,5},{5,4},{6,7},{7,6},{8,9},{9,8},{10,11... | collective-permute-start | bytes 516104 | tf_op jit(solution)/shard_map/ppermute | solution.py:168
  24.0 1.2 %collective-permute-start.5 = (f32[42,8,128]{2,1,0:T(8,128)S(1)}, f32[42,8,128]{2,1,0:T(8,128)S(1)}, u32[]{:S(2)}, u32[]{:S(2)}) collective-permute-start(f32[42,8,128]{2,1,0:T(8,128)S(1)} %get-tuple-element.75), channel_id=1, source_target_pairs={{1,2},{2,1},{0,3},{3,0},{5,6},{6,5},{4,7},{7,4},{9,10},{10,9},{8,1... | collective-permute-start | bytes 516104 | tf_op jit(solution)/shard_map/ppermute | solution.py:172
  25.2 0.0 copy-start.7
  25.2 0.0 copy-start.8
  25.2 0.0 copy-start.9
  25.3 3.8 %outer_forward_kernel.1 = (f32[76,72,128]{2,1,0:T(8,128)S(1)}, f32[76,72,128]{2,1,0:T(8,128)S(1)}, f32[76,72,128]{2,1,0:T(8,128)S(1)}, f32[76,72,128]{2,1,0:T(8,...) custom-call(f32[76,72,128]{2,1,0:T(8,128)S(1)} %get-tuple-element.69, ...), custom_call_target="tpu_custom_call", output_to_operand_aliasing={{0}: (2, {}), {1}: (3, {}), {2}: (4, {}), {3}: (5, {}), {4}... | custom-call | flops 16777216 | bytes 16777216 | tf_op jit(solution)/shard_map/outer_forward_kernel/pallas_call | solution.py:737
  29.1 0.0 copy-start
  29.1 0.0 collective-permute-done.4.za
  29.1 1.0 %collective-permute-done.5.zb = f32[42,8,128]{2,1,0:T(8,128)S(1)} collective-permute-done((f32[42,8,128]{2,1,0:T(8,128)S(1)}, f32[42,8,128]{2,1,0:T(8,128)S(1)}, u32[]{:S(2)}, u32[]{:S(2)}) %collective-permute-start.5) | collective-permute-done | bytes 172064 | tf_op jit(solution)/shard_map/ppermute | solution.py:172
  30.1 1.9 %edge_forward_kernel.1 = (f32[11,72,128]{2,1,0:T(8,128)S(1)}, f32[11,72,128]{2,1,0:T(8,128)S(1)}, f32[11,72,128]{2,1,0:T(8,128)S(1)}, f32[11,72,128]{2,1,0:T(8,1...) custom-call(f32[11,72,128]{2,1,0:T(8,128)S(1)} %get-tuple-element.73, ...), custom_call_target="tpu_custom_call", output_to_operand_aliasing={{0}: (0, {}), {1}: (1, {})} | custom-call | tf_op jit(solution)/shard_map/edge_forward_kernel/pallas_call | solution.py:737
  32.0 0.0 copy-done.7
  32.0 0.0 copy-done.8
  32.0 0.0 copy-done.9
  32.0 2.0 %middle_kernel.1 = (f32[76,72,128]{2,1,0:T(8,128)S(1)}, f32[8,64,128]{2,1,0:T(8,128)S(1)}, f32[32,8,128]{2,1,0:T(8,128)S(1)}, f32[32,8,128]{2,1,0:T(8,128)S(1)}) custom-call(f32[76,72,128]{2,1,0:T(8,128)S(1)} %get-tuple-element.72.u4, f32[11,72,128]{2,1,0:T(8,128)S(1)} %get-tuple-element.76.e4, ...), custom_call_target="tpu_custom_call", output_to_operand_aliasing={{0}: (0, {})} | custom-call | tf_op jit(solution)/shard_map/middle_kernel/pallas_call | solution.py:737
  34.1 0.4 collective-permute-start.8
  34.4 0.0 collective-permute-start.6
  34.4 3.4 %collective-permute-start.7 = (f32[32,8,128]{2,1,0:T(8,128)S(1)}, f32[32,8,128]{2,1,0:T(8,128)S(1)}, u32[]{:S(2)}, u32[]{:S(2)}) collective-permute-start(f32[32,8,128]{2,1,0:T(8,128)S(1)} %get-tuple-element.78), channel_id=1, source_target_pairs={{4,8},{8,4},{0,0},{12,12},{5,9},{9,5},{1,1},{13,13},{6,10},{10,6},... | collective-permute-start | bytes 393224 | tf_op jit(solution)/shard_map/ppermute | solution.py:172
  37.9 0.0 copy-done
  37.9 5.5 %_lambda_.3 = (f32[76,72,128]{2,1,0:T(8,128)S(1)}, f32[76,72,128]{2,1,0:T(8,128)S(1)}, f32[76,72,128]{2,1,0:T(8,128)S(1)}, f32[76,72,128]{2,1,0:T(8,128)S(1)}) custom-call(f32[76,72,128]{2,1,0:T(8,128)S(1)} %get-tuple-element.79.refs_0_, f32[76,72,128]{2,1,0:T(8,128)S(1)} %get-tuple-element.80.refs_1_, f32[76,72,128]{2,1,0:T(8,128)S(1)} %get-tuple-element.81.refs_2_, ...), custom_call_target="tpu_custom_call" | custom-call | flops 16777216 | bytes 16777216 | tf_op jit(solution)/shard_map/<lambda>/pallas_call | solution.py:737
  43.4 0.0 collective-permute-done.6.ya.args_3_
  43.4 0.0 collective-permute-done.7.yb.args_4_
  43.4 0.7 collective-permute-start.9
  44.1 5.4 %later_back.1 = (f32[76,72,128]{2,1,0:T(8,128)S(1)}, f32[76,72,128]{2,1,0:T(8,128)S(1)}, f32[76,72,128]{2,1,0:T(8,128)S(1)}, f32[76,72,128]{2,1,0:T(8,128)S(1)}) custom-call(f32[8,8,128]{2,1,0:T(8,128)S(1)} %corner_kernel.3.mark, f32[76,72,128]{2,1,0:T(8,128)S(1)} %get-tuple-element.79.refs_0_, ...), custom_call_target="tpu_custom_call", output_to_operand_aliasing={{2}: (8, {}), {3}: (9, {})} | custom-call | flops 16777216 | bytes 16777216 | tf_op jit(solution)/shard_map/later_back/pallas_call | solution.py:737
  49.4 0.0 collective-permute-done.9.args_5_.args_6_
  49.5 0.0 collective-permute-done.8.args_1_.args_2_
  49.5 0.0 copy-start.1
  49.5 1.7 %turn_kernel.1 = (f32[76,72,128]{2,1,0:T(8,128)S(1)}, f32[11,72,128]{2,1,0:T(8,128)S(1)}, f32[21,8,128]{2,1,0:T(8,128)S(1)}) custom-call(f32[76,72,128]{2,1,0:T(8,128)S(1)} %get-tuple-element.91.args_0_.refs_11_, f32[8,64,128]{2,1,0:T(8,128)S(1)} %collective-permute-done.8.args_1_.args_2_, ...), custom_call_target="tpu_custom_call", output_to_operand_aliasing={{0}: (7, {})} | custom-call | tf_op jit(solution)/shard_map/turn_kernel/pallas_call | solution.py:737
  51.2 1.1 %collective-permute-start.10 = (f32[21,8,128]{2,1,0:T(8,128)S(1)}, f32[21,8,128]{2,1,0:T(8,128)S(1)}, u32[]{:S(2)}, u32[]{:S(2)}) collective-permute-start(f32[21,8,128]{2,1,0:T(8,128)S(1)} %get-tuple-element.101), channel_id=1, source_target_pairs={{0,1},{1,0},{2,3},{3,2},{4,5},{5,4},{6,7},{7,6},{8,9},{9,8},{10,11... | collective-permute-start | bytes 258056 | tf_op jit(solution)/shard_map/ppermute | solution.py:168
  52.2 1.2 %collective-permute-start.11 = (f32[21,8,128]{2,1,0:T(8,128)S(1)}, f32[21,8,128]{2,1,0:T(8,128)S(1)}, u32[]{:S(2)}, u32[]{:S(2)}) collective-permute-start(f32[21,8,128]{2,1,0:T(8,128)S(1)} %get-tuple-element.101), channel_id=1, source_target_pairs={{1,2},{2,1},{0,3},{3,0},{5,6},{6,5},{4,7},{7,4},{9,10},{10,9},{8,1... | collective-permute-start | bytes 258056 | tf_op jit(solution)/shard_map/ppermute | solution.py:172
  53.4 0.0 copy-done.1
  53.4 4.9 %outer_backward_kernel.1 = (f32[76,72,128]{2,1,0:T(8,128)S(1)}, f32[76,72,128]{2,1,0:T(8,128)S(1)}, f32[76,72,128]{2,1,0:T(8,128)S(1)}, f32[76,72,128]{2,1,0:T(8...) custom-call(f32[76,72,128]{2,1,0:T(8,128)S(1)} %get-tuple-element.93, ...), custom_call_target="tpu_custom_call", output_to_operand_aliasing={{0}: (9, {}), {1}: (10, {}), {2}: (11, {}), {3}: (12, {}), ... | custom-call | flops 33554432 | bytes 33554432 | tf_op jit(solution)/shard_map/outer_backward_kernel/pallas_call | solution.py:737
  58.3 0.0 copy-start.2
  58.3 1.5 %copy-done.2 = f32[76,72,128]{2,1,0:T(8,128)} copy-done((f32[76,72,128]{2,1,0:T(8,128)}, f32[76,72,128]{2,1,0:T(8,128)S(1)}, u32[]{:S(2)}) %copy-start.2) | copy-done | bytes 2801688
  59.8 0.0 collective-permute-done.10.za
  59.8 0.0 copy-start.3
  59.8 0.0 collective-permute-done.11.zb
  59.8 2.5 %edge_backward_kernel.1 = (f32[11,72,128]{2,1,0:T(8,128)S(1)}, f32[11,72,128]{2,1,0:T(8,128)S(1)}) custom-call(f32[11,72,128]{2,1,0:T(8,128)S(1)} %get-tuple-element.100.lam, f32[21,8,128]{2,1,0:T(8,128)S(1)} %collective-permute-done.10.za, f32[21,8,128]{2,1,0:T(8,128)S(1)} %collective-permute-done.11.zb, f32[11,72,128]{2,1,0:T(8,128)S(1)} %get-tuple-element.102.u0, ...), custom_call_target="tpu_custom_call" | custom-call | tf_op jit(solution)/shard_map/edge_backward_kernel/pallas_call | solution.py:737
  62.3 0.0 copy-done.3
  62.3 3.8 %finish_kernel.1 = (f32[32,64,256]{2,1,0:T(8,128)}, f32[32,64,256]{2,1,0:T(8,128)}) custom-call(f32[4]{0:T(128)S(1)} %copy-done.10, s32[32,64,256]{2,1,0:T(8,128)S(1)} %copy-done.4, f32[76,72,128]{2,1,0:T(8,128)S(1)} %copy-done.3, f32[76,72,128]{2,1,0:T(8,128)S(1)} %get-tuple-element.98.acc, f32[76,72,128]{2,1,0:T(8,128)S(1)} %get-tuple-element.99.az, ...), custom_call_target="tpu_custom_call" | custom-call | tf_op jit(solution)/shard_map/finish_kernel/pallas_call | solution.py:737
  (2 shorter events, 0.0 us)
Async XLA Ops:
  0.6 8.0 %copy-start.4 = (s32[32,64,256]{2,1,0:T(8,128)S(1)}, s32[32,64,256]{2,1,0:T(8,128)}, u32[]{:S(2)}) copy-start(s32[32,64,256]{2,1,0:T(8,128)} %labels.5) | copy-start | bytes 6291460
  0.6 8.0 %copy-start.5 = (f32[32,64,256]{2,1,0:T(8,128)S(1)}, f32[32,64,256]{2,1,0:T(8,128)}, u32[]{:S(2)}) copy-start(f32[32,64,256]{2,1,0:T(8,128)} %u0.3) | copy-start | bytes 6291460
  0.7 8.0 %copy-start.6 = (f32[32,64,256]{2,1,0:T(8,128)S(1)}, f32[32,64,256]{2,1,0:T(8,128)}, u32[]{:S(2)}) copy-start(f32[32,64,256]{2,1,0:T(8,128)} %diffusivity.3) | copy-start | bytes 6291460
  0.7 8.0 %copy-start.10 = (f32[4]{0:T(128)S(1)}, f32[4]{0:T(128)}, u32[]{:S(2)}) copy-start(f32[4]{0:T(128)} %scale.5) | copy-start | bytes 52
  2.9 15.3 %collective-permute-start.2 = (f32[16,64,128]{2,1,0:T(8,128)S(1)}, f32[16,64,128]{2,1,0:T(8,128)S(1)}, u32[]{:S(2)}, u32[]{:S(2)}) collective-permute-start(f32[16,64,128]{2,1,0:T(8,128)S(1)} %get-tuple-element.67), channel_id=1, source_target_pairs={{0,16},{16,0},{1,17},{17,1},{2,18},{18,2},{3,19},{19,3},{4,20},{20... | collective-permute-start | bytes 1572872 | tf_op jit(solution)/shard_map/ppermute | solution.py:168
  4.1 10.8 %collective-permute-start = (f32[64,8,128]{2,1,0:T(8,128)S(1)}, f32[64,8,128]{2,1,0:T(8,128)S(1)}, u32[]{:S(2)}, u32[]{:S(2)}) collective-permute-start(f32[64,8,128]{2,1,0:T(8,128)S(1)} %get-tuple-element.57), channel_id=1, source_target_pairs={{0,4},{4,0},{8,12},{12,8},{1,5},{5,1},{9,13},{13,9},{2,6},{6,2},{1... | collective-permute-start | bytes 786440 | tf_op jit(solution)/shard_map/ppermute | solution.py:168
  4.3 10.6 %collective-permute-start.1 = (f32[64,8,128]{2,1,0:T(8,128)S(1)}, f32[64,8,128]{2,1,0:T(8,128)S(1)}, u32[]{:S(2)}, u32[]{:S(2)}) collective-permute-start(f32[64,8,128]{2,1,0:T(8,128)S(1)} %get-tuple-element.58), channel_id=1, source_target_pairs={{4,8},{8,4},{0,0},{12,12},{5,9},{9,5},{1,1},{13,13},{6,10},{10,6},... | collective-permute-start | bytes 786440 | tf_op jit(solution)/shard_map/ppermute | solution.py:172
  15.0 3.2 %collective-permute-start.3 = (f32[16,8,128]{2,1,0:T(8,128)S(1)}, f32[16,8,128]{2,1,0:T(8,128)S(1)}, u32[]{:S(2)}, u32[]{:S(2)}) collective-permute-start(f32[16,8,128]{2,1,0:T(8,128)S(1)} %corner_kernel.2.mark), channel_id=1, source_target_pairs={{0,16},{16,0},{1,17},{17,1},{2,18},{18,2},{3,19},{19,3},{4,20},{20... | collective-permute-start | bytes 196616 | tf_op jit(solution)/shard_map/ppermute | solution.py:168
  21.3 7.8 %collective-permute-start.4 = (f32[42,8,128]{2,1,0:T(8,128)S(1)}, f32[42,8,128]{2,1,0:T(8,128)S(1)}, u32[]{:S(2)}, u32[]{:S(2)}) collective-permute-start(f32[42,8,128]{2,1,0:T(8,128)S(1)} %get-tuple-element.75), channel_id=1, source_target_pairs={{0,1},{1,0},{2,3},{3,2},{4,5},{5,4},{6,7},{7,6},{8,9},{9,8},{10,11... | collective-permute-start | bytes 516104 | tf_op jit(solution)/shard_map/ppermute | solution.py:168
  24.0 6.1 %collective-permute-start.5 = (f32[42,8,128]{2,1,0:T(8,128)S(1)}, f32[42,8,128]{2,1,0:T(8,128)S(1)}, u32[]{:S(2)}, u32[]{:S(2)}) collective-permute-start(f32[42,8,128]{2,1,0:T(8,128)S(1)} %get-tuple-element.75), channel_id=1, source_target_pairs={{1,2},{2,1},{0,3},{3,0},{5,6},{6,5},{4,7},{7,4},{9,10},{10,9},{8,1... | collective-permute-start | bytes 516104 | tf_op jit(solution)/shard_map/ppermute | solution.py:172
  25.2 6.8 %copy-start.7 = (f32[32,64,256]{2,1,0:T(8,128)S(1)}, f32[32,64,256]{2,1,0:T(8,128)}, u32[]{:S(2)}) copy-start(f32[32,64,256]{2,1,0:T(8,128)} %measured.1) | copy-start | bytes 6291460
  25.2 6.8 %copy-start.8 = (s32[32,64,256]{2,1,0:T(8,128)S(1)}, s32[32,64,256]{2,1,0:T(8,128)}, u32[]{:S(2)}) copy-start(s32[32,64,256]{2,1,0:T(8,128)} %observed.1) | copy-start | bytes 6291460
  25.2 6.8 %copy-start.9 = (f32[32,64,256]{2,1,0:T(8,128)S(1)}, f32[32,64,256]{2,1,0:T(8,128)}, u32[]{:S(2)}) copy-start(f32[32,64,256]{2,1,0:T(8,128)} %adjoint.1) | copy-start | bytes 6291460
  29.1 8.8 %copy-start = (f32[76,72,128]{2,1,0:T(8,128)}, f32[76,72,128]{2,1,0:T(8,128)S(1)}, u32[]{:S(2)}) copy-start(f32[76,72,128]{2,1,0:T(8,128)S(1)} %get-tuple-element.84.refs_5_.refs_6_) | copy-start | bytes 8404996
  34.1 15.4 %collective-permute-start.8 = (f32[8,64,128]{2,1,0:T(8,128)S(1)}, f32[8,64,128]{2,1,0:T(8,128)S(1)}, u32[]{:S(2)}, u32[]{:S(2)}) collective-permute-start(f32[8,64,128]{2,1,0:T(8,128)S(1)} %get-tuple-element.92), channel_id=1, source_target_pairs={{0,16},{16,0},{1,17},{17,1},{2,18},{18,2},{3,19},{19,3},{4,20},{20... | collective-permute-start | bytes 786440 | tf_op jit(solution)/shard_map/ppermute | solution.py:168
  34.4 8.9 %collective-permute-start.6 = (f32[32,8,128]{2,1,0:T(8,128)S(1)}, f32[32,8,128]{2,1,0:T(8,128)S(1)}, u32[]{:S(2)}, u32[]{:S(2)}) collective-permute-start(f32[32,8,128]{2,1,0:T(8,128)S(1)} %get-tuple-element.77), channel_id=1, source_target_pairs={{0,4},{4,0},{8,12},{12,8},{1,5},{5,1},{9,13},{13,9},{2,6},{6,2},{1... | collective-permute-start | bytes 393224 | tf_op jit(solution)/shard_map/ppermute | solution.py:168
  34.4 8.9 %collective-permute-start.7 = (f32[32,8,128]{2,1,0:T(8,128)S(1)}, f32[32,8,128]{2,1,0:T(8,128)S(1)}, u32[]{:S(2)}, u32[]{:S(2)}) collective-permute-start(f32[32,8,128]{2,1,0:T(8,128)S(1)} %get-tuple-element.78), channel_id=1, source_target_pairs={{4,8},{8,4},{0,0},{12,12},{5,9},{9,5},{1,1},{13,13},{6,10},{10,6},... | collective-permute-start | bytes 393224 | tf_op jit(solution)/shard_map/ppermute | solution.py:172
  43.4 6.0 %collective-permute-start.9 = (f32[8,8,128]{2,1,0:T(8,128)S(1)}, f32[8,8,128]{2,1,0:T(8,128)S(1)}, u32[]{:S(2)}, u32[]{:S(2)}) collective-permute-start(f32[8,8,128]{2,1,0:T(8,128)S(1)} %corner_kernel.3.mark), channel_id=1, source_target_pairs={{0,16},{16,0},{1,17},{17,1},{2,18},{18,2},{3,19},{19,3},{4,20},{20... | collective-permute-start | bytes 98312 | tf_op jit(solution)/shard_map/ppermute | solution.py:168
  49.5 4.0 %copy-start.1 = (f32[76,72,128]{2,1,0:T(8,128)S(1)}, f32[76,72,128]{2,1,0:T(8,128)}, u32[]{:S(2)}) copy-start(f32[76,72,128]{2,1,0:T(8,128)} %copy-done) | copy-start | bytes 8404996
  51.2 8.7 %collective-permute-start.10 = (f32[21,8,128]{2,1,0:T(8,128)S(1)}, f32[21,8,128]{2,1,0:T(8,128)S(1)}, u32[]{:S(2)}, u32[]{:S(2)}) collective-permute-start(f32[21,8,128]{2,1,0:T(8,128)S(1)} %get-tuple-element.101), channel_id=1, source_target_pairs={{0,1},{1,0},{2,3},{3,2},{4,5},{5,4},{6,7},{7,6},{8,9},{9,8},{10,11... | collective-permute-start | bytes 258056 | tf_op jit(solution)/shard_map/ppermute | solution.py:168
  52.2 7.6 %collective-permute-start.11 = (f32[21,8,128]{2,1,0:T(8,128)S(1)}, f32[21,8,128]{2,1,0:T(8,128)S(1)}, u32[]{:S(2)}, u32[]{:S(2)}) collective-permute-start(f32[21,8,128]{2,1,0:T(8,128)S(1)} %get-tuple-element.101), channel_id=1, source_target_pairs={{1,2},{2,1},{0,3},{3,0},{5,6},{6,5},{4,7},{7,4},{9,10},{10,9},{8,1... | collective-permute-start | bytes 258056 | tf_op jit(solution)/shard_map/ppermute | solution.py:172
  58.3 1.5 %copy-start.2 = (f32[76,72,128]{2,1,0:T(8,128)}, f32[76,72,128]{2,1,0:T(8,128)S(1)}, u32[]{:S(2)}) copy-start(f32[76,72,128]{2,1,0:T(8,128)S(1)} %get-tuple-element.97.lam) | copy-start | bytes 8404996
  59.8 2.5 %copy-start.3 = (f32[76,72,128]{2,1,0:T(8,128)S(1)}, f32[76,72,128]{2,1,0:T(8,128)}, u32[]{:S(2)}) copy-start(f32[76,72,128]{2,1,0:T(8,128)} %copy-done.2) | copy-start | bytes 8404996

commit v2 on v1

--- a/solution.py
+++ b/solution.py
@@ -68,20 +68,14 @@
 
 def ahead(values):
     rolled = [pltpu.roll(v, 127, axis=1) for v in values]
-    count = len(values)
-    if count == 1:
-        return rolled
     last = lanes() == 127
-    return [jnp.where(last, rolled[(t + 1) % count], rolled[t]) for t in range(count)]
+    return [jnp.where(last, b, a) for a, b in zip(rolled, rolled[1:])] + rolled[-1:]
 
 
 def behind(values):
     rolled = [pltpu.roll(v, 1, axis=1) for v in values]
-    count = len(values)
-    if count == 1:
-        return rolled
     first = lanes() == 0
-    return [jnp.where(first, rolled[(t - 1) % count], rolled[t]) for t in range(count)]
+    return rolled[:1] + [jnp.where(first, a, b) for a, b in zip(rolled, rolled[1:])]
 
 
 class Plan:
@@ -101,7 +95,7 @@
         self.own_tiles = [OWN + 8 * t for t in range(self.ny // 8)]
         self.end_tiles = [self.row_tiles[0], self.row_tiles[-1]]
         self.edge_vregs = self.per_group * len(self.row_tiles)
-        self.face_vregs = -(-self.edge_vregs // 4)
+        self.face_vregs = -(-self.edge_vregs // 8)
 
     def index(self, axis):
         return lax.axis_index(axis)
@@ -272,11 +266,12 @@
             field[(plan.planes - 1) * nt + t] = zero
 
 
-def pack_edges(plan, field, edge, row_tiles):
+def pack_edges(plan, field, edge, row_tiles, first, count):
     nt = plan.tiles
     masks = [lanes() >= 16 * j for j in range(2 * GROUPS)]
 
-    def body(i, _):
+    for j in range(count):
+        i = first + j
         for row in row_tiles:
             value = None
             for g in range(GROUPS):
@@ -286,43 +281,50 @@
                 value = right if value is None else jnp.where(masks[2 * g], right, value)
                 value = jnp.where(masks[2 * g + 1], left, value)
             edge[i + 1, pl.ds(row, 8), :] = value
-        return 0
-
-    lax.fori_loop(0, plan.per_group, body, 0)
+
+
+def pack_halo_edges(plan, field, edge):
+    pack_edges(plan, field, edge, plan.end_tiles, 0, plan.per_group)
+    last = plan.per_group - HALO
+    starts = [0, last] if plan.two_sided else [jnp.where(plan.even("gx"), last, 0)]
+    for start in starts:
+        pack_edges(plan, field, edge, plan.row_tiles[1:-1], start, HALO)
 
 
 def edge_places(plan):
     return [(i + 1, row) for i in range(plan.per_group) for row in plan.row_tiles]
 
 
-def pack_faces(plan, edge, out, base):
-    lane = lanes()
+def pack_faces(plan, edge, first, second, base):
+    pos = lanes() % BLOCK
+    even = plan.even("gz")
     places = edge_places(plan)
     for q in range(plan.face_vregs):
-        value = None
-        for slot, (i, row) in enumerate(places[4 * q : 4 * q + 4]):
+        low = high = None
+        for slot, (i, row) in enumerate(places[8 * q : 8 * q + 8]):
             held = edge[i, pl.ds(row, 8), :]
-            low = pltpu.roll(held, (8 * slot - 20) % 128, axis=1)
-            high = pltpu.roll(held, (8 * slot - 4) % 128, axis=1)
-            both = jnp.where(lane % 8 < 4, low, high)
-            value = both if value is None else jnp.where(lane % BLOCK >= 8 * slot, both, value)
-        out[base + q] = value
+            a = pltpu.roll(held, (4 * slot - 20) % 128, axis=1)
+            b = pltpu.roll(held, (4 * slot - 8) % 128, axis=1)
+            low = a if low is None else jnp.where(pos >= 4 * slot, a, low)
+            high = b if high is None else jnp.where(pos >= 4 * slot, b, high)
+        first[base + q] = jnp.where(even, high, low)
+        second[base + q] = jnp.where(even, low, high)
 
 
 def place_faces(plan, edge, za, zb, base):
-    lane = lanes()
-    pos = lane % BLOCK
-    halo = (pos >= 12) & (pos < 20)
+    pos = lanes() % BLOCK
+    at_right, at_left = (pos >= 12) & (pos < 16), (pos >= 16) & (pos < 20)
     even = plan.even("gz")
     places = edge_places(plan)
     for q in range(plan.face_vregs):
         a, b = za[base + q], zb[base + q]
         right = jnp.where(plan.last("gz"), 0.0, jnp.where(even, a, b))
         left = jnp.where(plan.first("gz"), 0.0, jnp.where(even, b, a))
-        both = jnp.where(lane % 8 < 4, right, left)
-        for slot, (i, row) in enumerate(places[4 * q : 4 * q + 4]):
-            moved = pltpu.roll(both, (12 - 8 * slot) % 128, axis=1)
-            edge[i, pl.ds(row, 8), :] = jnp.where(halo, moved, edge[i, pl.ds(row, 8), :])
+        for slot, (i, row) in enumerate(places[8 * q : 8 * q + 8]):
+            value = edge[i, pl.ds(row, 8), :]
+            value = jnp.where(at_right, pltpu.roll(right, (12 - 4 * slot) % 128, axis=1), value)
+            value = jnp.where(at_left, pltpu.roll(left, (16 - 4 * slot) % 128, axis=1), value)
+            edge[i, pl.ds(row, 8), :] = value
 
 
 def wrap_planes(plan, edge):
@@ -349,20 +351,36 @@
 
 
 def face_coefficients(k, c, start, count, rows, tiles, unroll):
-    cx, cy, cz, czm = c
+    cx, cy, cz, czm, *own = c
 
     def body(i, _):
-        for j in range(unroll):
-            x = start + i * unroll + j
-            for row in rows:
-                here = load(k, x, row, tiles)
-                store(cx, x, row, add(here, load(k, x + 1, row, tiles)))
-                store(cy, x, row, add(here, load(k, x, row + 1, tiles)))
-                store(cz, x, row, add(here, ahead(here)))
-                store(czm, x, row, add(here, behind(here)))
+        for row in rows:
+            x = start + i * unroll
+            here = load(k, x, row, tiles)
+            low = add(here, load(k, x - 1, row, tiles))
+            for j in range(unroll):
+                x = start + i * unroll + j
+                next_ = load(k, x + 1, row, tiles)
+                high = add(here, next_)
+                up = add(here, load(k, x, row + 1, tiles))
+                down = add(here, load(k, x, row - 1, tiles))
+                right, left = add(here, ahead(here)), add(here, behind(here))
+                store(cx, x, row, high)
+                store(cy, x, row, up)
+                store(cz, x, row, right)
+                store(czm, x, row, left)
+                if own:
+                    whole = add(add(add(low, high), add(up, down)), add(right, left))
+                    store(own[0], x, row, [1.0 - value for value in whole])
+                here, low = next_, high
         return 0
 
     repeat(body, count // unroll)
+
+
+def low_faces(k, cx, plane, rows, tiles):
+    for row in rows:
+        store(cx, plane, row, add(load(k, plane, row, tiles), load(k, plane + 1, row, tiles)))
 
 
 def repeat(body, count):
@@ -381,35 +399,38 @@
     return [jnp.where(mask, value, 0.0) for value in total]
 
 
-def step_forward(v, w, c, start, count, rows, tiles, masks, plane_keep, unroll):
-    cx, cy, cz, czm = c
-
-    def body(i, _):
-        first = start + i * unroll
-        for row in rows:
-            here = load(v, first, row, tiles)
-            flow = mul(load(cx, first - 1, row, tiles), sub(here, load(v, first - 1, row, tiles)))
-            for k in range(unroll):
-                x = first + k
-                after = load(v, x + 1, row, tiles)
-                out = mul(load(cx, x, row, tiles), sub(after, here))
-                total = add(here, sub(out, flow))
+def step_forward(v, w, c, start, count, rows, tiles, masks, plane_keep):
+    cx, cy, cz, czm, *own = c
+    for row in rows:
+        before, here = load(v, start - 1, row, tiles), load(v, start, row, tiles)
+        low, flow = load(cx, start - 1, row, tiles), None
+        for j in range(count):
+            x = start + j
+            after, high = load(v, x + 1, row, tiles), load(cx, x, row, tiles)
+            above, below = load(cy, x, row, tiles), load(cy, x, row - 1, tiles)
+            right, left = load(cz, x, row, tiles), load(czm, x, row, tiles)
+            if own:
+                total = add(mul(low, before), mul(high, after))
+                total = add(total, add(mul(above, load(v, x, row + 1, tiles)), mul(below, load(v, x, row - 1, tiles))))
+                total = add(total, mul(load(own[0], x, row, tiles), here))
+                total = add(total, add(mul(right, ahead(here)), mul(left, behind(here))))
+            else:
+                out = mul(high, sub(after, here))
+                into = mul(low, sub(here, before)) if flow is None else flow
                 flow = out
-                up = mul(load(cy, x, row, tiles), sub(load(v, x, row + 1, tiles), here))
-                down = mul(load(cy, x, row - 1, tiles), sub(here, load(v, x, row - 1, tiles)))
+                total = add(here, sub(out, into))
+                up = mul(above, sub(load(v, x, row + 1, tiles), here))
+                down = mul(below, sub(here, load(v, x, row - 1, tiles)))
                 total = add(total, sub(up, down))
-                right = mul(load(cz, x, row, tiles), sub(ahead(here), here))
-                left = mul(load(czm, x, row, tiles), sub(here, behind(here)))
+                right, left = mul(right, sub(ahead(here), here)), mul(left, sub(here, behind(here)))
                 total = add(total, sub(right, left))
-                store(w, x, row, kept(total, masks[row], plane_keep, x))
-                here = after
-        return 0
-
-    repeat(body, count // unroll)
+            total = kept(total, masks[row], plane_keep, x)
+            store(w, x, row, total)
+            before, here, low = here, after, high
 
 
 def step_backward(v, w, u, sums, c, start, count, rows, tiles, masks, plane_keep, unroll, fresh):
-    cx, cy, cz, czm = c
+    cx, cy, cz, czm = c[:4]
     acc, az = sums
 
     def body(i, _):
@@ -444,7 +465,8 @@
                 total = add(total, sub(right, left))
                 term = mul(diff, sub(ahead(temp), temp))
                 store(az, x, row, term if fresh else add(term, load(az, x, row, tiles)))
-                store(w, x, row, kept(total, masks[row], plane_keep, x))
+                total = kept(total, masks[row], plane_keep, x)
+                store(w, x, row, total)
                 here, temp = after, temp_after
         return 0
 
@@ -479,49 +501,62 @@
     return out
 
 
-def face_kernel(plan, scale, u0, diffusivity, labels, px, pya, pyb, *rest):
-    *px2, scale_s, ux, dx, lx, uy, dy, ly, sems = rest
-    nt, ny = plan.tiles, plan.ny
-    even_x, even_y = plan.even("gx"), plan.even("gy")
+def read(copies):
+    for copy in copies:
+        copy.start()
+    for copy in copies:
+        copy.wait()
+
+
+def scaled(diffusivity, labels, values):
+    return diffusivity * factor_of(labels, values) * HALF_RATE
+
+
+def x_face_kernel(plan, scale, u0, diffusivity, labels, *refs):
+    *outs, scale_s, ux, dx, lx, sems = refs
+    nt = plan.tiles
+    even = plan.even("gx")
     low, high = 0, plan.nx - HALO
-    starts = [jnp.where(even_x, high, low)] + ([jnp.where(even_x, low, high)] if plan.two_sided else [])
+    starts = [jnp.where(even, high, low)] + ([jnp.where(even, low, high)] if plan.two_sided else [])
     copies = [pltpu.make_async_copy(scale, scale_s, sems.at[0])]
     for s, at in enumerate(starts):
         for n, (source, held) in enumerate(((u0, ux), (diffusivity, dx), (labels, lx))):
             copies.append(pltpu.make_async_copy(source.at[pl.ds(at, HALO)], held.at[s], sems.at[1 + 3 * s + n]))
-    for s, at in enumerate((0, ny - 8)):
-        for n, (source, held) in enumerate(((u0, uy), (diffusivity, dy), (labels, ly))):
-            copies.append(
-                pltpu.make_async_copy(source.at[:, pl.ds(at, 8), :], held.at[s], sems.at[7 + 3 * s + n])
-            )
-    for copy in copies:
-        copy.start()
-    for copy in copies:
-        copy.wait()
+    read(copies)
     values = [scale_s[m] for m in range(MATERIALS)]
-    wide = HALO * nt
-    for s, out in enumerate((px, *px2)):
+    for s, out in enumerate(outs):
         for j in range(HALO):
             for t in range(nt):
                 cols = pl.ds(128 * t, 128)
                 out[j * nt + t] = ux[s, j, :, cols]
-                out[wide + j * nt + t] = dx[s, j, :, cols] * factor_of(lx[s, j, :, cols], values) * HALF_RATE
+                out[(HALO + j) * nt + t] = scaled(dx[s, j, :, cols], lx[s, j, :, cols], values)
+
+
+def y_face_kernel(plan, scale, u0, diffusivity, labels, pya, pyb, scale_s, uy, dy, ly, sems):
+    nt = plan.tiles
+    even = plan.even("gy")
+    copies = [pltpu.make_async_copy(scale, scale_s, sems.at[0])]
+    for s, at in enumerate((0, plan.ny - 8)):
+        for n, (source, held) in enumerate(((u0, uy), (diffusivity, dy), (labels, ly))):
+            copies.append(pltpu.make_async_copy(source.at[:, pl.ds(at, 8), :], held.at[s], sems.at[1 + 3 * s + n]))
+    read(copies)
+    values = [scale_s[m] for m in range(MATERIALS)]
 
     def body(x, _):
         for t in range(nt):
             cols = pl.ds(128 * t, 128)
-            k = [dy[s, x, :, cols] * factor_of(ly[s, x, :, cols], values) * HALF_RATE for s in range(2)]
+            k = [scaled(dy[s, x, :, cols], ly[s, x, :, cols], values) for s in range(2)]
             u = [uy[s, x, :, cols] for s in range(2)]
             for f, (a, b) in enumerate((u, k)):
                 a, b = a[:HALO], b[8 - HALO :]
-                pya[x * nt + t, pl.ds(HALO * f, HALO), :] = jnp.where(even_y, b, a)
-                pyb[x * nt + t, pl.ds(HALO * f, HALO), :] = jnp.where(even_y, a, b)
+                pya[x * nt + t, pl.ds(HALO * f, HALO), :] = jnp.where(even, b, a)
+                pyb[x * nt + t, pl.ds(HALO * f, HALO), :] = jnp.where(even, a, b)
         return 0
 
     lax.fori_loop(0, plan.nx, body, 0, unroll=4)
 
 
-def own_kernel(plan, scale, u0, diffusivity, labels, u, k, cx, cy, cz, czm):
+def own_kernel(plan, scale, u0, diffusivity, labels, u, k, *c):
     nt = plan.tiles
     own = plan.own_plane()
     values = [scale[m] for m in range(MATERIALS)]
@@ -532,49 +567,51 @@
             cols = pl.ds(128 * t, 128)
             u[(own + x) * nt + t, pl.ds(OWN, plan.ny), :] = u0[x, :, cols]
             k[(own + x) * nt + t, pl.ds(OWN, plan.ny), :] = (
-                diffusivity[x, :, cols] * factor_of(labels[x, :, cols], values) * HALF_RATE
+                scaled(diffusivity[x, :, cols], labels[x, :, cols], values)
             )
         return 0
 
     lax.fori_loop(0, plan.nx, body, 0, unroll=2)
-    face_coefficients(k, (cx, cy, cz, czm), own - 1, plan.nx + 1, plan.own_tiles, nt, 3)
+    face_coefficients(k, c, own, plan.nx, plan.own_tiles, nt, 4)
+    low_faces(k, c[0], own - 1, plan.own_tiles, nt)
 
 
 def inner_forward_kernel(plan, steps, sources, *refs):
-    c, fields = refs[:4], refs[4:]
+    c, fields = refs[:5], refs[5:]
     clear_ends(plan, fields[sources:])
     masks = dict.fromkeys(plan.own_tiles)
     start, count = plan.core()
     for n, step in enumerate(steps):
         v, w = fields[sources - 1 + n], fields[sources + n]
-        step_forward(v, w, c, start, count, plan.own_tiles, plan.tiles, masks, None, inner_unroll(count))
+        step_forward(v, w, c, start, count, plan.own_tiles, plan.tiles, masks, None)
         for at, many in plan.strips(step):
-            step_forward(v, w, c, at, many, plan.own_tiles, plan.tiles, masks, None, many)
-
-
-def ready_kernel(plan, xa, xb, ya, yb, ca, cb, u_in, k_in, u, k, eu, ek, pz):
-    del u_in, k_in
+            step_forward(v, w, c, at, many, plan.own_tiles, plan.tiles, masks, None)
+
+
+def ready_kernel(plan, xa, xb, ya, yb, ca, cb, u_in, k_in, eu_in, ek_in, u, k, eu, ek, pza, pzb):
+    del u_in, k_in, eu_in, ek_in
     place_halos(plan, (u, k), xa, xb, ya, yb, ca, cb)
-    pack_edges(plan, u, eu, plan.row_tiles)
-    pack_edges(plan, k, ek, plan.row_tiles)
-    pack_faces(plan, eu, pz, 0)
-    pack_faces(plan, ek, pz, plan.face_vregs)
+    pack_halo_edges(plan, u, eu)
+    pack_halo_edges(plan, k, ek)
+    pack_faces(plan, eu, pza, pzb, 0)
+    pack_faces(plan, ek, pza, pzb, plan.face_vregs)
 
 
 def outer_forward_kernel(plan, u, k, *refs):
     c, later = refs[8:12], refs[12:]
     nt = plan.tiles
     own = plan.own_plane()
-    face_coefficients(k, c, own - 1, plan.nx + 1, plan.end_tiles, nt, 11)
-    for at, many in plan.beside(-HALO - 1, plan.nx - HALO - 1, 2 * HALO + 1):
-        face_coefficients(k, c, at, many, plan.row_tiles, nt, 3)
+    face_coefficients(k, c, own, plan.nx, plan.end_tiles, nt, 8)
+    low_faces(k, c[0], own - 1, plan.end_tiles, nt)
+    for at, many in plan.beside(-HALO, plan.nx - HALO, 2 * HALO):
+        face_coefficients(k, c, at, many, plan.row_tiles, nt, 4)
     fields = (u, *later)
     masks, keeper = plan.masks(), plane_keeper(plan)
     start, count = plan.core()
     for n in range(ITERS):
-        step_forward(fields[n], fields[n + 1], c, start, count, plan.end_tiles, nt, masks, None, 2 * inner_unroll(count))
+        step_forward(fields[n], fields[n + 1], c, start, count, plan.end_tiles, nt, masks, None)
         for at, many in plan.rims(n):
-            step_forward(fields[n], fields[n + 1], c, at, many, plan.row_tiles, nt, masks, keeper, many)
+            step_forward(fields[n], fields[n + 1], c, at, many, plan.row_tiles, nt, masks, keeper)
 
 
 def edge_masks(plan):
@@ -582,19 +619,20 @@
     return {row: keep if mask is None else keep & mask for row, mask in plan.masks().items()}
 
 
-def edge_forward_kernel(plan, eu, k_in, za, zb, e0, k, u1, u2, u3, u4, cx, cy, cz, czm):
+def edge_forward_kernel(plan, eu, k_in, za, zb, e0, k, u1, u2, u3, u4, *c):
     del eu, k_in
     place_faces(plan, e0, za, zb, 0)
     place_faces(plan, k, za, zb, plan.face_vregs)
     wrap_planes(plan, e0)
     wrap_planes(plan, k)
-    c = (cx, cy, cz, czm)
-    face_coefficients(k, c, 0, plan.per_group + 1, plan.row_tiles, 1, plan.per_group + 1)
+    face_coefficients(k, c, 1, plan.per_group, plan.row_tiles, 1, plan.per_group)
+    low_faces(k, c[0], 0, plan.row_tiles, 1)
     masks, keeper = edge_masks(plan), edge_keeper(plan)
     fields = (e0, u1, u2, u3, u4)
     for n in range(ITERS):
-        step_forward(fields[n], fields[n + 1], c, 1, plan.per_group, plan.row_tiles, 1, masks, keeper, plan.per_group)
-        wrap_planes(plan, fields[n + 1])
+        step_forward(fields[n], fields[n + 1], c, 1, plan.per_group, plan.row_tiles, 1, masks, keeper)
+        if n < ITERS - 1:
+            wrap_planes(plan, fields[n + 1])
 
 
 def edge_keeper(plan):
@@ -643,14 +681,14 @@
             inner_unroll(count), fresh and n == 0,
         )
         for at, many in plan.strips(step):
-            step_forward(v, w, c, at, many, plan.own_tiles, plan.tiles, masks, None, many)
-
-
-def turn_kernel(plan, xa, xb, ya, yb, ca, cb, lam_in, lam, edge, pz):
+            step_forward(v, w, c, at, many, plan.own_tiles, plan.tiles, masks, None)
+
+
+def turn_kernel(plan, xa, xb, ya, yb, ca, cb, lam_in, lam, edge, pza, pzb):
     del lam_in
     place_halos(plan, (lam,), xa, xb, ya, yb, ca, cb)
-    pack_edges(plan, lam, edge, plan.row_tiles)
-    pack_faces(plan, edge, pz, 0)
+    pack_edges(plan, lam, edge, plan.row_tiles, 0, plan.per_group)
+    pack_faces(plan, edge, pza, pzb, 0)
 
 
 def outer_backward_kernel(plan, lam, *refs):
@@ -695,15 +733,26 @@
     own = plan.own_plane()
     values = [scale[m] for m in range(MATERIALS)]
     chunk = 4
+    count, slots = plan.nx // chunk, grad_s.shape[0]
 
     def copies(i):
-        at = pl.ds(i * chunk, chunk)
+        at, slot = pl.ds(i * chunk, chunk), lax.rem(i, slots)
         return (
-            pltpu.make_async_copy(grad_s.at[at], gradient.at[at], sems.at[0, i]),
-            pltpu.make_async_copy(adj_s.at[at], adjoint.at[at], sems.at[1, i]),
+            pltpu.make_async_copy(grad_s.at[slot], gradient.at[at], sems.at[0, slot]),
+            pltpu.make_async_copy(adj_s.at[slot], adjoint.at[at], sems.at[1, slot]),
         )
 
+    def drain(i):
+        for copy in copies(i):
+            copy.wait()
+
     def body(i, _):
+        slot = lax.rem(i, slots)
+
+        @pl.when(i >= slots)
+        def _():
+            drain(i - slots)
+
         for j in range(chunk):
             x = i * chunk + j
             p = own + x
@@ -714,20 +763,16 @@
                 end = merge_edges(plan, load(lam, p, row, nt), e_lam, p, row)
                 for t in range(nt):
                     at = (x, pl.ds(row - OWN, 8), pl.ds(128 * t, 128))
-                    grad_s[at] = total[t] * (-HALF_RATE) * factor_of(labels[at], values)
-                    adj_s[at] = end[t]
+                    to = (slot, j, *at[1:])
+                    grad_s[to] = total[t] * (-HALF_RATE) * factor_of(labels[at], values)
+                    adj_s[to] = end[t]
         for copy in copies(i):
             copy.start()
         return 0
 
-    lax.fori_loop(0, plan.nx // chunk, body, 0)
-
-    def drain(i, _):
-        for copy in copies(i):
-            copy.wait()
-        return 0
-
-    lax.fori_loop(0, plan.nx // chunk, drain, 0)
+    lax.fori_loop(0, count, body, 0)
+    for i in range(max(count - slots, 0), count):
+        drain(jnp.int32(i))
 
 
 def call(kernel, outs, args, alias=None, scratch=(), smem=0, flops=0, specs=None, out_spec=in_vmem, mib=3):
@@ -774,13 +819,15 @@
         return (xa, xb, ya, yb, ca, cb), got[0]
 
     hbm = [pltpu.with_memory_space_constraint(a, pltpu.HBM) for a in (material_scale, checkpoint, diffusivity, labels)]
-    held = [vm(sides, HALO, ny, nz)] * 2 + [pltpu.VMEM((sides, HALO, ny, nz), jnp.int32)]
-    held += [vm(2, nx, 8, nz)] * 2 + [pltpu.VMEM((2, nx, 8, nz), jnp.int32)]
-    sent = call(
-        part(face_kernel, plan), faces(2), hbm, specs=[anywhere] * 4, mib=8,
-        scratch=[pltpu.SMEM((MATERIALS,), F32), *held, pltpu.SemaphoreType.DMA((13,))],
-    )
-    u, k, *c = call(part(own_kernel, plan), (work,) * 6, (material_scale, checkpoint, diffusivity, labels), smem=1, flops=1 << 23)
+    def face_call(kernel, outs, *shape):
+        scratch = [pltpu.SMEM((MATERIALS,), F32), vm(*shape), vm(*shape), pltpu.VMEM(shape, jnp.int32)]
+        scratch += [pltpu.SemaphoreType.DMA((1 + 3 * shape[0],))]
+        return call(part(kernel, plan), outs, hbm, specs=[anywhere] * 4, mib=5, scratch=scratch)
+
+    px, pya, pyb, *px2 = faces(2)
+    px, *px2 = face_call(x_face_kernel, (px, *px2), sides, HALO, ny, nz)
+    sent = (px, *face_call(y_face_kernel, (pya, pyb), 2, nx, 8, nz), *px2)
+    u, k, *c = call(part(own_kernel, plan), (work,) * 7, (material_scale, checkpoint, diffusivity, labels), smem=1, flops=1 << 23)
     state = {}
 
     def first_half():
@@ -792,23 +839,27 @@
     got, mark = exchange(2, sent, first_half)
     u1, u2 = state["new"]
 
-    def later_half(mark, *refs):
+    def later_half(mark, u, k, *refs):
         del mark
+        *refs, eu, ek = refs
         inner_forward_kernel(plan, (2, 3), 1, *refs)
-
-    u3, u4 = call(part(later_half), (work,) * 2, (mark, *c, u2), flops=1 << 23)
-    u, k, eu, ek, pz = call(
-        part(after(ready_kernel), plan), (work, work, edge, edge, vm(2 * plan.face_vregs, 8, 128)),
-        (u4, *got, u, k), alias={7: 0, 8: 1},
+        pack_edges(plan, u, eu, plan.row_tiles, 0, plan.per_group)
+        pack_edges(plan, k, ek, plan.row_tiles, 0, plan.per_group)
+
+    u3, u4, eu, ek = call(part(later_half), (work, work, edge, edge), (mark, u, k, *c, u2), flops=1 << 23)
+    lanes_sent = vm(2 * plan.face_vregs, 8, 128)
+    u, k, eu, ek, pza, pzb = call(
+        part(after(ready_kernel), plan), (work, work, edge, edge, lanes_sent, lanes_sent),
+        (u4, *got, u, k, eu, ek), alias={7 + i: i for i in range(4)},
     )
-    za, zb = swap(plan, "gz", pz, pz, True)
+    za, zb = swap(plan, "gz", pza, pzb, True)
     out = call(
-        part(outer_forward_kernel, plan), (work,) * 8, (u, k, *c, u1, u2, u3, u4),
+        part(outer_forward_kernel, plan), (work,) * 8, (u, k, *c[:4], u1, u2, u3, u4),
         alias={2 + i: i for i in range(8)}, flops=1 << 24,
     )
     c, (u1, u2, u3, u4) = out[:4], out[4:]
-    e0, _, e1, e2, e3, e4, ex, ey, ez, ezm = call(
-        part(edge_forward_kernel, plan), (edge,) * 10, (eu, ek, za, zb), alias={0: 0, 1: 1}
+    e0, _, e1, e2, e3, e4, ex, ey, ez, ezm, _ = call(
+        part(edge_forward_kernel, plan), (edge,) * 11, (eu, ek, za, zb), alias={0: 0, 1: 1}
     )
     lam, *sent = call(
         part(middle_kernel, plan), (work,) + faces(1), (u4, e4, measured, observed, adjoint_in), alias={0: 0}
@@ -831,10 +882,11 @@
     l1, l0, acc, az = call(
         part(later_back), (work,) * 4, (mark, *c, u1, u, l2, acc, az), alias={8: 2, 9: 3}, flops=1 << 24
     )
-    lam, e_lam, pz = call(
-        part(after(turn_kernel), plan), (work, edge, vm(plan.face_vregs, 8, 128)), (l0, *got, lam), alias={7: 0}
+    lanes_sent = vm(plan.face_vregs, 8, 128)
+    lam, e_lam, pza, pzb = call(
+        part(after(turn_kernel), plan), (work, edge, lanes_sent, lanes_sent), (l0, *got, lam), alias={7: 0}
     )
-    za, zb = swap(plan, "gz", pz, pz, True)
+    za, zb = swap(plan, "gz", pza, pzb, True)
     l3, l2, l1, l0, acc, az = call(
         part(outer_backward_kernel, plan), (work,) * 6, (lam, *c, u, u1, u2, u3, l3, l2, l1, l0, acc, az),
         alias={9 + i: i for i in range(6)}, flops=1 << 25,
@@ -845,7 +897,7 @@
     block = jax.ShapeDtypeStruct((nx, ny, nz), F32)
     return call(
         part(finish_kernel, plan), (block, block), (material_scale, labels, l0, acc, az, e_start, e_total), smem=1,
-        out_spec=anywhere, mib=6, scratch=[vm(nx, ny, nz), vm(nx, ny, nz), pltpu.SemaphoreType.DMA((2, nx // 4))],
+        out_spec=anywhere, mib=4, scratch=[vm(4, 4, ny, nz), vm(4, 4, ny, nz), pltpu.SemaphoreType.DMA((2, 4))],
     )
 
 

time: 66.9 us -> 62.4 us (0.933)
  Pallas kernels: 45.8 us -> 44.1 us
  local copies, waits for them, and re-layouts: 1.56 us -> 0.04 us
    pallas_call x16 -> x17, Pallas kernels: 45.8 us -> 44.1 us  [call(): pl.pallas_call(kernel, out_shape=tuple(outs), in_specs=specs, out_specs=(...]
    unnamed x22 -> x18, local copies, waits for them, and re-layouts: 1.56 us -> 0.04 us
  transfers between devices with their start and end apart: 12 -> 12, of which waited for: 2 -> 1; matrix products, arithmetic and copies ran while one was open for 0% -> 0% of each run, Pallas kernels for 43% -> 48%
where the time goes in v2:
time: 62.4 us; the launch traced here: 62.2 us
  Pallas kernels  44.1 us (71%)
  starting transfers between devices  16.5 us (26%)
  between operations  1.13 us (2%)
    pallas_call x17, Pallas kernels, call(): pl.pallas_call(kernel, out_shape=tuple(outs), in_specs=specs, out_specs=(...  44.1 us
    ppermute x4, starting transfers between devices, swap(): return (got, lax.ppermute(second, axis, pairs(count, True) + ends))  9.8 us
    ppermute x8, starting transfers between devices, swap(): got = lax.ppermute(first, axis, pairs(count, False))  6.65 us
  transfers between devices with their start and end apart: 12, of which 1 were waited for; matrix products, arithmetic and copies ran while one was open for 0% of the time, Pallas kernels for 48%

profile of v2, /device:TPU:9, one launch (start us, length us, event | category | flops | bytes accessed | tf_op | source)
XLA Modules:
  0.0 62.2 jit_solution(13138238235490184490)
XLA Ops:
  0.6 1.2 %x_face_kernel.1 = f32[16,64,128]{2,1,0:T(8,128)S(1)} custom-call(f32[4]{0:T(128)} %scale.7, f32[32,64,256]{2,1,0:T(8,128)} %u0.5, f32[32,64,256]{2,1,0:T(8,128)} %diffusivity.5, s32[32,64,256]{2,1,0:T(8,128)} %labels.7), custom_call_target="tpu_custom_call" | custom-call | tf_op jit(solution)/shard_map/x_face_kernel/pallas_call | solution.py:782
  1.9 0.0 copy-start.2
  1.9 0.0 copy-start.3
  1.9 0.0 copy-start.4
  1.9 0.0 copy-start.8
  1.9 1.3 %collective-permute-start.2 = (f32[16,64,128]{2,1,0:T(8,128)S(1)}, f32[16,64,128]{2,1,0:T(8,128)S(1)}, u32[]{:S(2)}, u32[]{:S(2)}) collective-permute-start(f32[16,64,128]{2,1,0:T(8,128)S(1)} %x_face_kernel.1), channel_id=1, source_target_pairs={{0,16},{16,0},{1,17},{17,1},{2,18},{18,2},{3,19},{19,3},{4,20},{20... | collective-permute-start | bytes 1572872 | tf_op jit(solution)/shard_map/ppermute | solution.py:162
  3.2 2.2 %y_face_kernel.1 = (f32[64,8,128]{2,1,0:T(8,128)S(1)}, f32[64,8,128]{2,1,0:T(8,128)S(1)}) custom-call(f32[4]{0:T(128)} %scale.7, f32[32,64,256]{2,1,0:T(8,128)} %u0.5, f32[32,64,256]{2,1,0:T(8,128)} %diffusivity.5, s32[32,64,256]{2,1,0:T(8,128)} %labels.7), custom_call_target="tpu_custom_call" | custom-call | tf_op jit(solution)/shard_map/y_face_kernel/pallas_call | solution.py:782
  5.4 0.1 collective-permute-start
  5.5 4.5 %collective-permute-start.1 = (f32[64,8,128]{2,1,0:T(8,128)S(1)}, f32[64,8,128]{2,1,0:T(8,128)S(1)}, u32[]{:S(2)}, u32[]{:S(2)}) collective-permute-start(f32[64,8,128]{2,1,0:T(8,128)S(1)} %get-tuple-element.62), channel_id=1, source_target_pairs={{4,8},{8,4},{0,0},{12,12},{5,9},{9,5},{1,1},{13,13},{6,10},{10,6},... | collective-permute-start | bytes 786440 | tf_op jit(solution)/shard_map/ppermute | solution.py:166
  10.0 0.0 copy-done.2
  10.0 0.0 copy-done.3
  10.0 0.0 copy-done.4
  10.0 0.0 copy-done.8
  10.0 2.9 %own_kernel.1 = (f32[76,72,128]{2,1,0:T(8,128)S(1)}, f32[76,72,128]{2,1,0:T(8,128)S(1)}, f32[76,72,128]{2,1,0:T(8,128)S(1)}, f32[76,72,128]{2,1,0:T(8,128)S(1)},...) custom-call(f32[4]{0:T(128)S(1)} %copy-done.8, f32[32,64,256]{2,1,0:T(8,128)S(1)} %copy-done.3, ...), custom_call_target="tpu_custom_call" | custom-call | flops 8388608 | bytes 8388608 | tf_op jit(solution)/shard_map/own_kernel/pallas_call | solution.py:782
  13.0 2.2 %_lambda_.2 = (f32[76,72,128]{2,1,0:T(8,128)S(1)}, f32[76,72,128]{2,1,0:T(8,128)S(1)}) custom-call(f32[76,72,128]{2,1,0:T(8,128)S(1)} %get-tuple-element.63.refs_0_, f32[76,72,128]{2,1,0:T(8,128)S(1)} %get-tuple-element.64.refs_1_, f32[76,72,128]{2,1,0:T(8,128)S(1)} %get-tuple-element.65.refs_2_, f32[76,72,128]{2,1,0:T(8,128)S(1)} %get-tuple-element.66.refs_3_, ...), custom_call_target="tpu_custom_call" | custom-call | flops 8388608 | bytes 8388608 | tf_op jit(solution)/shard_map/<lambda>/pallas_call | solution.py:782
  15.2 0.0 collective-permute-done.ya.args_3_
  15.2 0.5 collective-permute-done.1.yb.args_4_
  15.7 0.0 collective-permute-start.3
  15.7 3.5 %later_half.1 = (f32[76,72,128]{2,1,0:T(8,128)S(1)}, f32[76,72,128]{2,1,0:T(8,128)S(1)}, f32[11,72,128]{2,1,0:T(8,128)S(1)}, f32[11,72,128]{2,1,0:T(8,128)S(1)}) custom-call(f32[16,8,128]{2,1,0:T(8,128)S(1)} %corner_kernel.2.mark, f32[76,72,128]{2,1,0:T(8,128)S(1)} %get-tuple-element.68.refs_5_.u.args_7_, f32[76,72,128]{2,1,0:T(8,128)S(1)} %get-tuple-element.70.k.args_8_, ...), custom_call_target="tpu_custom_call" | custom-call | flops 8388608 | bytes 8388608 | tf_op jit(solution)/shard_map/later_half/pallas_call | solution.py:782
  19.2 0.0 collective-permute-done.3.args_5_.args_6_
  19.2 0.0 collective-permute-done.2.args_1_.args_2_
  19.2 1.4 %ready_kernel.1 = (f32[76,72,128]{2,1,0:T(8,128)S(1)}, f32[76,72,128]{2,1,0:T(8,128)S(1)}, f32[11,72,128]{2,1,0:T(8,128)S(1)}, f32[11,72,128]{2,1,0:T(8,128)S(1)...) custom-call(f32[76,72,128]{2,1,0:T(8,128)S(1)} %get-tuple-element.72, ...), custom_call_target="tpu_custom_call", output_to_operand_aliasing={{0}: (7, {}), {1}: (8, {}), {2}: (9, {}), {3}: (10, {})} | custom-call | tf_op jit(solution)/shard_map/ready_kernel/pallas_call | solution.py:782
  20.6 2.4 %collective-permute-start.4 = (f32[22,8,128]{2,1,0:T(8,128)S(1)}, f32[22,8,128]{2,1,0:T(8,128)S(1)}, u32[]{:S(2)}, u32[]{:S(2)}) collective-permute-start(f32[22,8,128]{2,1,0:T(8,128)S(1)} %get-tuple-element.81), channel_id=1, source_target_pairs={{0,1},{1,0},{2,3},{3,2},{4,5},{5,4},{6,7},{7,6},{8,9},{9,8},{10,11... | collective-permute-start | bytes 270344 | tf_op jit(solution)/shard_map/ppermute | solution.py:162
  23.0 1.2 %collective-permute-start.5 = (f32[22,8,128]{2,1,0:T(8,128)S(1)}, f32[22,8,128]{2,1,0:T(8,128)S(1)}, u32[]{:S(2)}, u32[]{:S(2)}) collective-permute-start(f32[22,8,128]{2,1,0:T(8,128)S(1)} %get-tuple-element.82), channel_id=1, source_target_pairs={{1,2},{2,1},{0,3},{3,0},{5,6},{6,5},{4,7},{7,4},{9,10},{10,9},{8,1... | collective-permute-start | bytes 270344 | tf_op jit(solution)/shard_map/ppermute | solution.py:166
  24.2 0.0 copy-start.5
  24.2 0.0 copy-start.6
  24.2 0.0 copy-start.7
  24.2 3.4 %outer_forward_kernel.1 = (f32[76,72,128]{2,1,0:T(8,128)S(1)}, f32[76,72,128]{2,1,0:T(8,128)S(1)}, f32[76,72,128]{2,1,0:T(8,128)S(1)}, f32[76,72,128]{2,1,0:T(8,...) custom-call(f32[76,72,128]{2,1,0:T(8,128)S(1)} %get-tuple-element.75, ...), custom_call_target="tpu_custom_call", output_to_operand_aliasing={{0}: (2, {}), {1}: (3, {}), {2}: (4, {}), {3}: (5, {}), {4}... | custom-call | flops 16777216 | bytes 16777216 | tf_op jit(solution)/shard_map/outer_forward_kernel/pallas_call | solution.py:782
  27.6 0.0 copy-start
  27.6 0.0 collective-permute-done.4.za
  27.6 0.0 collective-permute-done.5.zb
  27.6 1.9 %edge_forward_kernel.1 = (f32[11,72,128]{2,1,0:T(8,128)S(1)}, f32[11,72,128]{2,1,0:T(8,128)S(1)}, f32[11,72,128]{2,1,0:T(8,128)S(1)}, f32[11,72,128]{2,1,0:T(8,1...) custom-call(f32[11,72,128]{2,1,0:T(8,128)S(1)} %get-tuple-element.79, ...), custom_call_target="tpu_custom_call", output_to_operand_aliasing={{0}: (0, {}), {1}: (1, {})} | custom-call | tf_op jit(solution)/shard_map/edge_forward_kernel/pallas_call | solution.py:782
  29.6 0.0 copy-done.5
  29.6 0.0 copy-done.6
  29.6 0.0 copy-done.7
  29.6 2.1 %middle_kernel.1 = (f32[76,72,128]{2,1,0:T(8,128)S(1)}, f32[8,64,128]{2,1,0:T(8,128)S(1)}, f32[32,8,128]{2,1,0:T(8,128)S(1)}, f32[32,8,128]{2,1,0:T(8,128)S(1)}) custom-call(f32[76,72,128]{2,1,0:T(8,128)S(1)} %get-tuple-element.78.u4, f32[11,72,128]{2,1,0:T(8,128)S(1)} %get-tuple-element.83.e4, ...), custom_call_target="tpu_custom_call", output_to_operand_aliasing={{0}: (0, {})} | custom-call | tf_op jit(solution)/shard_map/middle_kernel/pallas_call | solution.py:782
  31.7 1.1 %collective-permute-start.8 = (f32[8,64,128]{2,1,0:T(8,128)S(1)}, f32[8,64,128]{2,1,0:T(8,128)S(1)}, u32[]{:S(2)}, u32[]{:S(2)}) collective-permute-start(f32[8,64,128]{2,1,0:T(8,128)S(1)} %get-tuple-element.99), channel_id=1, source_target_pairs={{0,16},{16,0},{1,17},{17,1},{2,18},{18,2},{3,19},{19,3},{4,20},{20... | collective-permute-start | bytes 786440 | tf_op jit(solution)/shard_map/ppermute | solution.py:162
  32.8 0.0 collective-permute-start.6
  32.8 3.5 %collective-permute-start.7 = (f32[32,8,128]{2,1,0:T(8,128)S(1)}, f32[32,8,128]{2,1,0:T(8,128)S(1)}, u32[]{:S(2)}, u32[]{:S(2)}) collective-permute-start(f32[32,8,128]{2,1,0:T(8,128)S(1)} %get-tuple-element.85), channel_id=1, source_target_pairs={{4,8},{8,4},{0,0},{12,12},{5,9},{9,5},{1,1},{13,13},{6,10},{10,6},... | collective-permute-start | bytes 393224 | tf_op jit(solution)/shard_map/ppermute | solution.py:166
  36.3 0.0 copy-done
  36.3 5.5 %_lambda_.3 = (f32[76,72,128]{2,1,0:T(8,128)S(1)}, f32[76,72,128]{2,1,0:T(8,128)S(1)}, f32[76,72,128]{2,1,0:T(8,128)S(1)}, f32[76,72,128]{2,1,0:T(8,128)S(1)}) custom-call(f32[76,72,128]{2,1,0:T(8,128)S(1)} %get-tuple-element.86.refs_0_, f32[76,72,128]{2,1,0:T(8,128)S(1)} %get-tuple-element.87.refs_1_, f32[76,72,128]{2,1,0:T(8,128)S(1)} %get-tuple-element.88.refs_2_, ...), custom_call_target="tpu_custom_call" | custom-call | flops 16777216 | bytes 16777216 | tf_op jit(solution)/shard_map/<lambda>/pallas_call | solution.py:782
  41.8 0.0 collective-permute-done.6.ya.args_3_
  41.8 0.0 collective-permute-done.7.yb.args_4_
  41.8 0.5 collective-permute-start.9
  42.4 5.5 %later_back.1 = (f32[76,72,128]{2,1,0:T(8,128)S(1)}, f32[76,72,128]{2,1,0:T(8,128)S(1)}, f32[76,72,128]{2,1,0:T(8,128)S(1)}, f32[76,72,128]{2,1,0:T(8,128)S(1)}) custom-call(f32[8,8,128]{2,1,0:T(8,128)S(1)} %corner_kernel.3.mark, f32[76,72,128]{2,1,0:T(8,128)S(1)} %get-tuple-element.86.refs_0_, ...), custom_call_target="tpu_custom_call", output_to_operand_aliasing={{2}: (8, {}), {3}: (9, {})} | custom-call | flops 16777216 | bytes 16777216 | tf_op jit(solution)/shard_map/later_back/pallas_call | solution.py:782
  47.8 0.0 collective-permute-done.9.args_5_.args_6_
  47.8 0.0 collective-permute-done.8.args_1_.args_2_
  47.8 0.0 copy-start.1
  47.9 1.1 %turn_kernel.1 = (f32[76,72,128]{2,1,0:T(8,128)S(1)}, f32[11,72,128]{2,1,0:T(8,128)S(1)}, f32[11,8,128]{2,1,0:T(8,128)S(1)}, f32[11,8,128]{2,1,0:T(8,128)S(1)}) custom-call(f32[76,72,128]{2,1,0:T(8,128)S(1)} %get-tuple-element.98.args_0_.refs_11_, f32[8,64,128]{2,1,0:T(8,128)S(1)} %collective-permute-done.8.args_1_.args_2_, ...), custom_call_target="tpu_custom_call", output_to_operand_aliasing={{0}: (7, {})} | custom-call | tf_op jit(solution)/shard_map/turn_kernel/pallas_call | solution.py:782
  49.0 1.4 %collective-permute-start.10 = (f32[11,8,128]{2,1,0:T(8,128)S(1)}, f32[11,8,128]{2,1,0:T(8,128)S(1)}, u32[]{:S(2)}, u32[]{:S(2)}) collective-permute-start(f32[11,8,128]{2,1,0:T(8,128)S(1)} %get-tuple-element.108), channel_id=1, source_target_pairs={{0,1},{1,0},{2,3},{3,2},{4,5},{5,4},{6,7},{7,6},{8,9},{9,8},{10,11... | collective-permute-start | bytes 135176 | tf_op jit(solution)/shard_map/ppermute | solution.py:162
  50.3 0.6 collective-permute-start.11
  50.9 0.0 copy-done.1
  50.9 4.9 %outer_backward_kernel.1 = (f32[76,72,128]{2,1,0:T(8,128)S(1)}, f32[76,72,128]{2,1,0:T(8,128)S(1)}, f32[76,72,128]{2,1,0:T(8,128)S(1)}, f32[76,72,128]{2,1,0:T(8...) custom-call(f32[76,72,128]{2,1,0:T(8,128)S(1)} %get-tuple-element.10, ...), custom_call_target="tpu_custom_call", output_to_operand_aliasing={{0}: (9, {}), {1}: (10, {}), {2}: (11, {}), {3}: (12, {}), ... | custom-call | flops 33554432 | bytes 33554432 | tf_op jit(solution)/shard_map/outer_backward_kernel/pallas_call | solution.py:782
  55.9 0.0 collective-permute-done.10.za
  55.9 0.0 collective-permute-done.11.zb
  55.9 2.5 %edge_backward_kernel.1 = (f32[11,72,128]{2,1,0:T(8,128)S(1)}, f32[11,72,128]{2,1,0:T(8,128)S(1)}) custom-call(f32[11,72,128]{2,1,0:T(8,128)S(1)} %get-tuple-element.107.lam, f32[11,8,128]{2,1,0:T(8,128)S(1)} %collective-permute-done.10.za, f32[11,8,128]{2,1,0:T(8,128)S(1)} %collective-permute-done.11.zb, f32[11,72,128]{2,1,0:T(8,128)S(1)} %get-tuple-element.110.u0, ...), custom_call_target="tpu_custom_call" | custom-call | tf_op jit(solution)/shard_map/edge_backward_kernel/pallas_call | solution.py:782
  58.3 3.7 %finish_kernel.1 = (f32[32,64,256]{2,1,0:T(8,128)}, f32[32,64,256]{2,1,0:T(8,128)}) custom-call(f32[4]{0:T(128)S(1)} %copy-done.8, s32[32,64,256]{2,1,0:T(8,128)S(1)} %copy-done.2, f32[76,72,128]{2,1,0:T(8,128)S(1)} %get-tuple-element.104.lam, f32[76,72,128]{2,1,0:T(8,128)S(1)} %get-tuple-element.105.acc, f32[76,72,128]{2,1,0:T(8,128)S(1)} %get-tuple-element.106.az, ...), custom_call_target="tpu_custom_call" | custom-call | tf_op jit(solution)/shard_map/finish_kernel/pallas_call | solution.py:782
  (2 shorter events, 0.0 us)
Async XLA Ops:
  1.9 8.1 %copy-start.2 = (s32[32,64,256]{2,1,0:T(8,128)S(1)}, s32[32,64,256]{2,1,0:T(8,128)}, u32[]{:S(2)}) copy-start(s32[32,64,256]{2,1,0:T(8,128)} %labels.7) | copy-start | bytes 6291460
  1.9 8.1 %copy-start.3 = (f32[32,64,256]{2,1,0:T(8,128)S(1)}, f32[32,64,256]{2,1,0:T(8,128)}, u32[]{:S(2)}) copy-start(f32[32,64,256]{2,1,0:T(8,128)} %u0.5) | copy-start | bytes 6291460
  1.9 8.1 %copy-start.4 = (f32[32,64,256]{2,1,0:T(8,128)S(1)}, f32[32,64,256]{2,1,0:T(8,128)}, u32[]{:S(2)}) copy-start(f32[32,64,256]{2,1,0:T(8,128)} %diffusivity.5) | copy-start | bytes 6291460
  1.9 8.1 %copy-start.8 = (f32[4]{0:T(128)S(1)}, f32[4]{0:T(128)}, u32[]{:S(2)}) copy-start(f32[4]{0:T(128)} %scale.7) | copy-start | bytes 52
  1.9 17.3 %collective-permute-start.2 = (f32[16,64,128]{2,1,0:T(8,128)S(1)}, f32[16,64,128]{2,1,0:T(8,128)S(1)}, u32[]{:S(2)}, u32[]{:S(2)}) collective-permute-start(f32[16,64,128]{2,1,0:T(8,128)S(1)} %x_face_kernel.1), channel_id=1, source_target_pairs={{0,16},{16,0},{1,17},{17,1},{2,18},{18,2},{3,19},{19,3},{4,20},{20... | collective-permute-start | bytes 1572872 | tf_op jit(solution)/shard_map/ppermute | solution.py:162
  5.4 9.7 %collective-permute-start = (f32[64,8,128]{2,1,0:T(8,128)S(1)}, f32[64,8,128]{2,1,0:T(8,128)S(1)}, u32[]{:S(2)}, u32[]{:S(2)}) collective-permute-start(f32[64,8,128]{2,1,0:T(8,128)S(1)} %get-tuple-element.61), channel_id=1, source_target_pairs={{0,4},{4,0},{8,12},{12,8},{1,5},{5,1},{9,13},{13,9},{2,6},{6,2},{1... | collective-permute-start | bytes 786440 | tf_op jit(solution)/shard_map/ppermute | solution.py:162
  5.5 10.2 %collective-permute-start.1 = (f32[64,8,128]{2,1,0:T(8,128)S(1)}, f32[64,8,128]{2,1,0:T(8,128)S(1)}, u32[]{:S(2)}, u32[]{:S(2)}) collective-permute-start(f32[64,8,128]{2,1,0:T(8,128)S(1)} %get-tuple-element.62), channel_id=1, source_target_pairs={{4,8},{8,4},{0,0},{12,12},{5,9},{9,5},{1,1},{13,13},{6,10},{10,6},... | collective-permute-start | bytes 786440 | tf_op jit(solution)/shard_map/ppermute | solution.py:166
  15.7 3.5 %collective-permute-start.3 = (f32[16,8,128]{2,1,0:T(8,128)S(1)}, f32[16,8,128]{2,1,0:T(8,128)S(1)}, u32[]{:S(2)}, u32[]{:S(2)}) collective-permute-start(f32[16,8,128]{2,1,0:T(8,128)S(1)} %corner_kernel.2.mark), channel_id=1, source_target_pairs={{0,16},{16,0},{1,17},{17,1},{2,18},{18,2},{3,19},{19,3},{4,20},{20... | collective-permute-start | bytes 196616 | tf_op jit(solution)/shard_map/ppermute | solution.py:162
  20.6 6.9 %collective-permute-start.4 = (f32[22,8,128]{2,1,0:T(8,128)S(1)}, f32[22,8,128]{2,1,0:T(8,128)S(1)}, u32[]{:S(2)}, u32[]{:S(2)}) collective-permute-start(f32[22,8,128]{2,1,0:T(8,128)S(1)} %get-tuple-element.81), channel_id=1, source_target_pairs={{0,1},{1,0},{2,3},{3,2},{4,5},{5,4},{6,7},{7,6},{8,9},{9,8},{10,11... | collective-permute-start | bytes 270344 | tf_op jit(solution)/shard_map/ppermute | solution.py:162
  23.0 4.6 %collective-permute-start.5 = (f32[22,8,128]{2,1,0:T(8,128)S(1)}, f32[22,8,128]{2,1,0:T(8,128)S(1)}, u32[]{:S(2)}, u32[]{:S(2)}) collective-permute-start(f32[22,8,128]{2,1,0:T(8,128)S(1)} %get-tuple-element.82), channel_id=1, source_target_pairs={{1,2},{2,1},{0,3},{3,0},{5,6},{6,5},{4,7},{7,4},{9,10},{10,9},{8,1... | collective-permute-start | bytes 270344 | tf_op jit(solution)/shard_map/ppermute | solution.py:166
  24.2 5.4 %copy-start.5 = (f32[32,64,256]{2,1,0:T(8,128)S(1)}, f32[32,64,256]{2,1,0:T(8,128)}, u32[]{:S(2)}) copy-start(f32[32,64,256]{2,1,0:T(8,128)} %measured.1) | copy-start | bytes 6291460
  24.2 5.4 %copy-start.6 = (s32[32,64,256]{2,1,0:T(8,128)S(1)}, s32[32,64,256]{2,1,0:T(8,128)}, u32[]{:S(2)}) copy-start(s32[32,64,256]{2,1,0:T(8,128)} %observed.1) | copy-start | bytes 6291460
  24.2 5.4 %copy-start.7 = (f32[32,64,256]{2,1,0:T(8,128)S(1)}, f32[32,64,256]{2,1,0:T(8,128)}, u32[]{:S(2)}) copy-start(f32[32,64,256]{2,1,0:T(8,128)} %adjoint.1) | copy-start | bytes 6291460
  27.6 8.7 %copy-start = (f32[76,72,128]{2,1,0:T(8,128)}, f32[76,72,128]{2,1,0:T(8,128)S(1)}, u32[]{:S(2)}) copy-start(f32[76,72,128]{2,1,0:T(8,128)S(1)} %get-tuple-element.91.refs_5_.refs_6_) | copy-start | bytes 8404996
  31.7 16.1 %collective-permute-start.8 = (f32[8,64,128]{2,1,0:T(8,128)S(1)}, f32[8,64,128]{2,1,0:T(8,128)S(1)}, u32[]{:S(2)}, u32[]{:S(2)}) collective-permute-start(f32[8,64,128]{2,1,0:T(8,128)S(1)} %get-tuple-element.99), channel_id=1, source_target_pairs={{0,16},{16,0},{1,17},{17,1},{2,18},{18,2},{3,19},{19,3},{4,20},{20... | collective-permute-start | bytes 786440 | tf_op jit(solution)/shard_map/ppermute | solution.py:162
  32.8 9.0 %collective-permute-start.6 = (f32[32,8,128]{2,1,0:T(8,128)S(1)}, f32[32,8,128]{2,1,0:T(8,128)S(1)}, u32[]{:S(2)}, u32[]{:S(2)}) collective-permute-start(f32[32,8,128]{2,1,0:T(8,128)S(1)} %get-tuple-element.84), channel_id=1, source_target_pairs={{0,4},{4,0},{8,12},{12,8},{1,5},{5,1},{9,13},{13,9},{2,6},{6,2},{1... | collective-permute-start | bytes 393224 | tf_op jit(solution)/shard_map/ppermute | solution.py:162
  32.8 9.0 %collective-permute-start.7 = (f32[32,8,128]{2,1,0:T(8,128)S(1)}, f32[32,8,128]{2,1,0:T(8,128)S(1)}, u32[]{:S(2)}, u32[]{:S(2)}) collective-permute-start(f32[32,8,128]{2,1,0:T(8,128)S(1)} %get-tuple-element.85), channel_id=1, source_target_pairs={{4,8},{8,4},{0,0},{12,12},{5,9},{9,5},{1,1},{13,13},{6,10},{10,6},... | collective-permute-start | bytes 393224 | tf_op jit(solution)/shard_map/ppermute | solution.py:166
  41.8 6.0 %collective-permute-start.9 = (f32[8,8,128]{2,1,0:T(8,128)S(1)}, f32[8,8,128]{2,1,0:T(8,128)S(1)}, u32[]{:S(2)}, u32[]{:S(2)}) collective-permute-start(f32[8,8,128]{2,1,0:T(8,128)S(1)} %corner_kernel.3.mark), channel_id=1, source_target_pairs={{0,16},{16,0},{1,17},{17,1},{2,18},{18,2},{3,19},{19,3},{4,20},{20... | collective-permute-start | bytes 98312 | tf_op jit(solution)/shard_map/ppermute | solution.py:162
  47.8 3.1 %copy-start.1 = (f32[76,72,128]{2,1,0:T(8,128)S(1)}, f32[76,72,128]{2,1,0:T(8,128)}, u32[]{:S(2)}) copy-start(f32[76,72,128]{2,1,0:T(8,128)} %copy-done) | copy-start | bytes 8404996
  49.0 6.9 %collective-permute-start.10 = (f32[11,8,128]{2,1,0:T(8,128)S(1)}, f32[11,8,128]{2,1,0:T(8,128)S(1)}, u32[]{:S(2)}, u32[]{:S(2)}) collective-permute-start(f32[11,8,128]{2,1,0:T(8,128)S(1)} %get-tuple-element.108), channel_id=1, source_target_pairs={{0,1},{1,0},{2,3},{3,2},{4,5},{5,4},{6,7},{7,6},{8,9},{9,8},{10,11... | collective-permute-start | bytes 135176 | tf_op jit(solution)/shard_map/ppermute | solution.py:162
  50.3 5.6 %collective-permute-start.11 = (f32[11,8,128]{2,1,0:T(8,128)S(1)}, f32[11,8,128]{2,1,0:T(8,128)S(1)}, u32[]{:S(2)}, u32[]{:S(2)}) collective-permute-start(f32[11,8,128]{2,1,0:T(8,128)S(1)} %get-tuple-element.109), channel_id=1, source_target_pairs={{1,2},{2,1},{0,3},{3,0},{5,6},{6,5},{4,7},{7,4},{9,10},{10,9},{8,1... | collective-permute-start | bytes 135176 | tf_op jit(solution)/shard_map/ppermute | solution.py:166
